TPU v7x, 1024 devices: a whole 4x4x32 slice. The times are simulated.
1024 devices in a mesh: seq: 128 (over z, x_lo, core), head: 8 (over x_hi, y).
Axes of the slice: x: 4 (x_hi: 2, x_lo: 2; x = x_hi * 2 + x_lo), y: 4, z: 32, core: 2. Of those that a mesh axis runs over, the one named last changes fastest.
Arguments:
- queries: bfloat16 [131072, 1024], P('seq', 'head'), may hold values from -16 to 16
- keys: bfloat16 [131072, 128], P(('seq', 'head')), may hold values from -4 to 4
- values: bfloat16 [131072, 128], P(('seq', 'head')), may hold values from -6 to 6
- doc_start: int32 [131072], P('seq'), may hold values from 0 to 131071, as said below
Outputs:
- attn_out: bfloat16 [131072, 1024], P('seq', 'head')
- lse: float32 [8, 131072], P('head', 'seq')
Inputs may be any that keep to these rules, and one draw needn't show every extreme that they name: doc_start[0] is 0, and for p >= 1 doc_start[p] is either p or doc_start[p - 1]; the first document covers at least the first 3072 tokens; the last token always begins a document of its own.
All inputs are finite; a program needn't handle non-finite values.
Results may differ from a plain program's by a relative error of at most 0.0045.
Values may be sent and summed in bfloat16 or wider, within the bound.
No kernel may reach another device: no remote copies, remote signals or barrier semaphores. Data moves between devices by JAX's collectives and lax.ppermute only.
A program may use at most 32 MiB of HBM per device.

v0:
```python
import math

import jax
import jax.numpy as jnp
from jax import lax
from jax.sharding import PartitionSpec as P

negative_fill = -1e30


def shifted(value, axis, steps):
    count = lax.axis_size(axis)
    initial, last = (max(0, -steps), min(count, count - steps))
    return lax.ppermute(value, axis, [(source, source + steps) for source in range(initial, last)])


def merge_tile(state, query_rows, key_rows, value_rows, visible, score_scale):
    run_max, run_sum, run_acc = state
    scores = (
        jnp.einsum("qhd,kd->hqk", query_rows, key_rows, preferred_element_type=jnp.float32)
        * score_scale
    )
    scores = jnp.where(visible[None], scores, negative_fill)
    new_max = jnp.maximum(run_max, jnp.max(scores, axis=-1))
    factor = jnp.exp(run_max - new_max)
    weights = jnp.where(visible[None], jnp.exp(scores - new_max[..., None]), 0.0)
    new_sum = run_sum * factor + jnp.sum(weights, axis=-1)
    rounded = weights.astype(jnp.bfloat16)
    new_acc = run_acc * factor[..., None] + jnp.einsum(
        "hqk,kd->hqd", rounded, value_rows, preferred_element_type=jnp.float32
    )
    return (new_max, new_sum, new_acc)


def body(queries, keys, values, doc_start):
    span = doc_start.shape[0]
    head_dim = keys.shape[1]
    head_count = queries.shape[1] // head_dim
    device_pos = lax.axis_index("seq")
    own_keys, own_values = (
        lax.all_gather(keys, "head", axis=0, tiled=True),
        lax.all_gather(values, "head", axis=0, tiled=True),
    )
    near_keys, near_values = shifted((own_keys, own_values), "seq", 1)
    far_keys, far_values = shifted((own_keys, own_values), "seq", 2)
    stops = ((own_keys, own_values), (near_keys, near_values), (far_keys, far_values))
    rows_block = min(512, span)
    block_count = span // rows_block
    score_scale = 1.0 / math.sqrt(head_dim)
    query_blocks = queries.reshape(block_count, rows_block, head_count, head_dim)
    start_blocks = doc_start.reshape(block_count, rows_block)
    offsets = jnp.arange(block_count, dtype=jnp.int32) * rows_block

    def attend_block(inputs):
        query_rows, start_rows, offset = inputs
        query_pos = device_pos * span + offset + jnp.arange(rows_block, dtype=jnp.int32)
        carry = (
            jnp.full((head_count, rows_block), negative_fill, jnp.float32),
            jnp.zeros((head_count, rows_block), jnp.float32),
            jnp.zeros((head_count, rows_block, head_dim), jnp.float32),
        )
        for stop_index in range(3):
            stop_keys, stop_values = stops[stop_index]
            key_base = (device_pos - stop_index) * span

            def key_step(
                kblock, state, stop_keys=stop_keys, stop_values=stop_values, key_base=key_base
            ):
                key_rows = lax.dynamic_slice_in_dim(stop_keys, kblock * rows_block, rows_block, 0)
                value_rows = lax.dynamic_slice_in_dim(
                    stop_values, kblock * rows_block, rows_block, 0
                )
                key_pos = key_base + kblock * rows_block + jnp.arange(rows_block, dtype=jnp.int32)
                visible = (key_pos[None, :] <= query_pos[:, None]) & (
                    key_pos[None, :] >= start_rows[:, None]
                )
                return merge_tile(state, query_rows, key_rows, value_rows, visible, score_scale)

            carry = lax.fori_loop(0, block_count, key_step, carry)
        run_max, run_sum, run_acc = carry
        normed = (
            (run_acc / run_sum[..., None])
            .transpose(1, 0, 2)
            .reshape(rows_block, head_count * head_dim)
        )
        return (normed.astype(jnp.bfloat16), run_max + jnp.log(run_sum))

    normed, log_total = lax.map(attend_block, (query_blocks, start_blocks, offsets))
    attn_out = normed.reshape(span, head_count * head_dim)
    lse = log_total.transpose(1, 0, 2).reshape(head_count, span)
    return (attn_out, lse)


def solution(mesh):
    in_specs = (P("seq", "head"), P(("seq", "head"), None), P(("seq", "head"), None), P("seq"))
    out_specs = (P("seq", "head"), P("head", "seq"))
    return jax.shard_map(body, mesh=mesh, in_specs=in_specs, out_specs=out_specs, check_vma=False)
```

profile of v0, /device:TPU:2, one launch (start us, length us, event | category | flops | bytes accessed | tf_op | source)
XLA Modules:
  0.0 115.8 jit_solution(10364425696487802688)
XLA Ops:
  0.6 34.8 %all_gather.6 = bf16[1024,128]{1,0:T(8,128)(2,1)S(1)} all-gather(bf16[128,128]{1,0:T(8,128)(2,1)} %param.13), channel_id=1, replica_groups=mesh['seq'=128,'head'=8] {'head'}, dimensions={0}, use_global_device_ids=true | all-gather | bytes 294912 | tf_op jit(solution)/shard_map/all_gather | solution.py:41
  35.4 1.9 %collective-permute-start = (bf16[1024,128]{1,0:T(8,128)(2,1)S(1)}, bf16[1024,128]{1,0:T(8,128)(2,1)S(1)}, u32[]{:S(2)}, u32[]{:S(2)}) collective-permute-start(bf16[1024,128]{1,0:T(8,128)(2,1)S(1)} %all_gather.6), channel_id=1, source_target_pairs={{0,8},{8,16},{16,24},{24,32},{32,40},{40,48},{48,56},{56,64},{64,7... | collective-permute-start | bytes 786440 | tf_op jit(solution)/shard_map/ppermute | solution.py:14
  37.3 34.5 %all_gather.7 = bf16[1024,128]{1,0:T(8,128)(2,1)S(1)} all-gather(bf16[128,128]{1,0:T(8,128)(2,1)S(1)} %copy-done.1), channel_id=1, replica_groups=mesh['seq'=128,'head'=8] {'head'}, dimensions={0}, use_global_device_ids=true | all-gather | bytes 294912 | tf_op jit(solution)/shard_map/all_gather | solution.py:42
  71.8 1.9 %collective-permute-start.1 = (bf16[1024,128]{1,0:T(8,128)(2,1)S(1)}, bf16[1024,128]{1,0:T(8,128)(2,1)S(1)}, u32[]{:S(2)}, u32[]{:S(2)}) collective-permute-start(bf16[1024,128]{1,0:T(8,128)(2,1)S(1)} %all_gather.7), channel_id=1, source_target_pairs={{0,8},{8,16},{16,24},{24,32},{32,40},{40,48},{48,56},{56,64},{64,7... | collective-permute-start | bytes 786440 | tf_op jit(solution)/shard_map/ppermute | solution.py:14
  73.7 4.5 %collective-permute-start.2 = (bf16[1024,128]{1,0:T(8,128)(2,1)S(1)}, bf16[1024,128]{1,0:T(8,128)(2,1)S(1)}, u32[]{:S(2)}, u32[]{:S(2)}) collective-permute-start(bf16[1024,128]{1,0:T(8,128)(2,1)S(1)} %all_gather.6), channel_id=1, source_target_pairs={{0,16},{8,24},{16,32},{24,40},{32,48},{40,56},{48,64},{56,72},{64,... | collective-permute-start | bytes 786440 | tf_op jit(solution)/shard_map/ppermute | solution.py:14
  78.2 4.9 %collective-permute-start.3 = (bf16[1024,128]{1,0:T(8,128)(2,1)S(1)}, bf16[1024,128]{1,0:T(8,128)(2,1)S(1)}, u32[]{:S(2)}, u32[]{:S(2)}) collective-permute-start(bf16[1024,128]{1,0:T(8,128)(2,1)S(1)} %all_gather.7), channel_id=1, source_target_pairs={{0,16},{8,24},{16,32},{24,40},{32,48},{40,56},{48,64},{56,72},{64,... | collective-permute-start | bytes 786440 | tf_op jit(solution)/shard_map/ppermute | solution.py:14
  83.2 0.7 copy-done.2
  83.9 7.7 %collective-permute-done.2 = bf16[1024,128]{1,0:T(8,128)(2,1)S(1)} collective-permute-done((bf16[1024,128]{1,0:T(8,128)(2,1)S(1)}, bf16[1024,128]{1,0:T(8,128)(2,1)S(1)}, u32[]{:S(2)}, u32[]{:S(2)}) %collective-permute-start.2) | collective-permute-done | bytes 262176 | tf_op jit(solution)/shard_map/ppermute | solution.py:14
  91.6 2.8 %collective-permute-done.3 = bf16[1024,128]{1,0:T(8,128)(2,1)S(1)} collective-permute-done((bf16[1024,128]{1,0:T(8,128)(2,1)S(1)}, bf16[1024,128]{1,0:T(8,128)(2,1)S(1)}, u32[]{:S(2)}, u32[]{:S(2)}) %collective-permute-start.3) | collective-permute-done | bytes 262176 | tf_op jit(solution)/shard_map/ppermute | solution.py:14
  94.5 20.7 %while.98 = (s32[]{:T(128)}, bf16[2,512,128]{2,1,0:T(8,128)(2,1)}, f32[2,1,512]{2,1,0:T(1,128)S(1)}, s32[2]{0:T(128)S(1)}, s32[]{:T(128)}, /*index=5*/s32[2,512]...) while((s32[]{:T(128)}, bf16[2,512,128]{2,1,0:T(8,128)(2,1)}, ...), condition=%wide.region_13.14_spmd, body=%wide.region_0.13_spmd.sunk | while | flops 417406976 | bytes 15121726 | solution.py:88
  94.5 0.6 dynamic_slice.97
  95.8 2.7 %while.99 = (s32[]{:T(128)}, f32[1,512]{1,0:T(1,128)S(1)}, f32[1,512]{1,0:T(1,128)S(1)}, f32[1,512,128]{2,1,0:T(8,128)S(1)}, s32[]{:T(128)}, /*index=5*/s32[512]...) while((s32[]{:T(128)}, f32[1,512]{1,0:T(1,128)S(1)}, ...), condition=%wide.region_4.4_spmd.clone, body=%wide.region_1.3_spmd.clone.sunk | while | flops 139136512 | bytes 4118747 | solution.py:79
  98.5 2.7 %while.100 = (s32[]{:T(128)}, f32[1,512]{1,0:T(1,128)S(1)}, f32[1,512]{1,0:T(1,128)S(1)}, f32[1,512,128]{2,1,0:T(8,128)S(1)}, s32[]{:T(128)}, /*index=5*/s32[512...) while((s32[]{:T(128)}, f32[1,512]{1,0:T(1,128)S(1)}, ...), condition=%wide.region_8.8_spmd.clone, body=%wide.region_5.7_spmd.clone.sunk | while | flops 139069440 | bytes 4118735 | solution.py:79
  99.3 0.6 fusion.97
  100.6 0.6 fusion.97
  101.2 2.7 %while.101 = (s32[]{:T(128)}, f32[1,512]{1,0:T(1,128)S(1)}, f32[1,512]{1,0:T(1,128)S(1)}, f32[1,512,128]{2,1,0:T(8,128)S(1)}, s32[]{:T(128)}, /*index=5*/s32[512...) while((s32[]{:T(128)}, f32[1,512]{1,0:T(1,128)S(1)}, ...), condition=%wide.region_12.12_spmd.clone, body=%wide.region_9.11_spmd.clone.sunk | while | flops 139069440 | bytes 4118735 | solution.py:79
  102.0 0.6 fusion.102
  104.1 0.7 copy-done.4
  104.8 0.6 dynamic_slice.97
  106.2 2.7 %while.99 = (s32[]{:T(128)}, f32[1,512]{1,0:T(1,128)S(1)}, f32[1,512]{1,0:T(1,128)S(1)}, f32[1,512,128]{2,1,0:T(8,128)S(1)}, s32[]{:T(128)}, /*index=5*/s32[512]...) while((s32[]{:T(128)}, f32[1,512]{1,0:T(1,128)S(1)}, ...), condition=%wide.region_4.4_spmd.clone, body=%wide.region_1.3_spmd.clone.sunk | while | flops 139136512 | bytes 4118747 | solution.py:79
  108.8 2.7 %while.100 = (s32[]{:T(128)}, f32[1,512]{1,0:T(1,128)S(1)}, f32[1,512]{1,0:T(1,128)S(1)}, f32[1,512,128]{2,1,0:T(8,128)S(1)}, s32[]{:T(128)}, /*index=5*/s32[512...) while((s32[]{:T(128)}, f32[1,512]{1,0:T(1,128)S(1)}, ...), condition=%wide.region_8.8_spmd.clone, body=%wide.region_5.7_spmd.clone.sunk | while | flops 139069440 | bytes 4118735 | solution.py:79
  111.6 2.7 %while.101 = (s32[]{:T(128)}, f32[1,512]{1,0:T(1,128)S(1)}, f32[1,512]{1,0:T(1,128)S(1)}, f32[1,512,128]{2,1,0:T(8,128)S(1)}, s32[]{:T(128)}, /*index=5*/s32[512...) while((s32[]{:T(128)}, f32[1,512]{1,0:T(1,128)S(1)}, ...), condition=%wide.region_12.12_spmd.clone, body=%wide.region_9.11_spmd.clone.sunk | while | flops 139069440 | bytes 4118735 | solution.py:79
  114.5 0.7 copy-done.4
  115.2 0.6 copy-done.5
  (113 shorter events, 14.3 us)
Async XLA Ops:
  0.6 36.7 %copy-start.1 = (bf16[128,128]{1,0:T(8,128)(2,1)S(1)}, bf16[128,128]{1,0:T(8,128)(2,1)}, u32[]{:S(2)}) copy-start(bf16[128,128]{1,0:T(8,128)(2,1)} %param.14) | copy-start | bytes 98308
  0.6 93.8 %copy-start = (bf16[1024,128]{1,0:T(8,128)(2,1)S(1)}, bf16[1024,128]{1,0:T(8,128)(2,1)}, u32[]{:S(2)}) copy-start(bf16[1024,128]{1,0:T(8,128)(2,1)} %param.12) | copy-start | bytes 786436
  35.4 48.5 %collective-permute-start = (bf16[1024,128]{1,0:T(8,128)(2,1)S(1)}, bf16[1024,128]{1,0:T(8,128)(2,1)S(1)}, u32[]{:S(2)}, u32[]{:S(2)}) collective-permute-start(bf16[1024,128]{1,0:T(8,128)(2,1)S(1)} %all_gather.6), channel_id=1, source_target_pairs={{0,8},{8,16},{16,24},{24,32},{32,40},{40,48},{48,56},{56,64},{64,7... | collective-permute-start | bytes 786440 | tf_op jit(solution)/shard_map/ppermute | solution.py:14
  71.8 12.1 %collective-permute-start.1 = (bf16[1024,128]{1,0:T(8,128)(2,1)S(1)}, bf16[1024,128]{1,0:T(8,128)(2,1)S(1)}, u32[]{:S(2)}, u32[]{:S(2)}) collective-permute-start(bf16[1024,128]{1,0:T(8,128)(2,1)S(1)} %all_gather.7), channel_id=1, source_target_pairs={{0,8},{8,16},{16,24},{24,32},{32,40},{40,48},{48,56},{56,64},{64,7... | collective-permute-start | bytes 786440 | tf_op jit(solution)/shard_map/ppermute | solution.py:14
  73.7 17.9 %collective-permute-start.2 = (bf16[1024,128]{1,0:T(8,128)(2,1)S(1)}, bf16[1024,128]{1,0:T(8,128)(2,1)S(1)}, u32[]{:S(2)}, u32[]{:S(2)}) collective-permute-start(bf16[1024,128]{1,0:T(8,128)(2,1)S(1)} %all_gather.6), channel_id=1, source_target_pairs={{0,16},{8,24},{16,32},{24,40},{32,48},{40,56},{48,64},{56,72},{64,... | collective-permute-start | bytes 786440 | tf_op jit(solution)/shard_map/ppermute | solution.py:14
  78.2 16.2 %collective-permute-start.3 = (bf16[1024,128]{1,0:T(8,128)(2,1)S(1)}, bf16[1024,128]{1,0:T(8,128)(2,1)S(1)}, u32[]{:S(2)}, u32[]{:S(2)}) collective-permute-start(bf16[1024,128]{1,0:T(8,128)(2,1)S(1)} %all_gather.7), channel_id=1, source_target_pairs={{0,16},{8,24},{16,32},{24,40},{32,48},{40,56},{48,64},{56,72},{64,... | collective-permute-start | bytes 786440 | tf_op jit(solution)/shard_map/ppermute | solution.py:14
  83.2 0.7 copy-start.2
  101.2 2.7 %copy-start.3 = (bf16[2,512,128]{2,1,0:T(8,128)(2,1)S(1)}, bf16[2,512,128]{2,1,0:T(8,128)(2,1)}, u32[]{:S(2)}) copy-start(bf16[2,512,128]{2,1,0:T(8,128)(2,1)} %get-tuple-element.1449) | copy-start | bytes 786436 | tf_op jit(solution)/shard_map/while
  104.1 0.7 copy-start.4
  111.5 2.7 %copy-start.3 = (bf16[2,512,128]{2,1,0:T(8,128)(2,1)S(1)}, bf16[2,512,128]{2,1,0:T(8,128)(2,1)}, u32[]{:S(2)}) copy-start(bf16[2,512,128]{2,1,0:T(8,128)(2,1)} %get-tuple-element.1449) | copy-start | bytes 786436 | tf_op jit(solution)/shard_map/while
  114.5 0.7 copy-start.4
  115.2 0.6 copy-start.5
where the time goes:
time: 116 us
  blocking collectives  69.2 us (60%)
  starting transfers between devices  13.3 us (11%)
  matrix products  11.2 us (10%)
  waiting for transfers between devices  10.5 us (9%)
  other arithmetic  4.56 us (4%)
  local copies, waits for them, and re-layouts  4.04 us (3%)
  loops' own time  2.18 us (2%)
    all_gather x1, blocking collectives, body(): lax.all_gather(keys, 'head', axis=0, tiled=True)  34.8 us
    all_gather x1, blocking collectives, body(): lax.all_gather(values, 'head', axis=0, tiled=True)  34.5 us
    ppermute x4, starting transfers between devices, shifted(): lax.ppermute(value, axis, [(source, source + steps) for source in range(i...  13.3 us
    ppermute x4, waiting for transfers between devices, shifted(): lax.ppermute(value, axis, [(source, source + steps) for source in range(i...  10.5 us
    dot_general x12, matrix products, merge_tile(): jnp.einsum('hqk,kd->hqd', rounded, value_rows, preferred_element_type=jnp...  6.6 us
    dot_general x12, matrix products, merge_tile(): jnp.einsum('qhd,kd->hqk', query_rows, key_rows, preferred_element_type=jn...  4.64 us
    reduce_sum x12, other arithmetic, merge_tile(): new_sum = run_sum * factor + jnp.sum(weights, axis=-1)  3.81 us
  transfers between devices with their start and end apart: 4, of which 2 were waited for; matrix products, arithmetic and copies ran while one was open for 0% of the time, Pallas kernels for 0%

commit v1 on v0

v1 whole, which is shorter than its diff:
```python
import functools
import math

import jax
import jax.numpy as jnp
from jax import lax
from jax.experimental import pallas as pl
from jax.experimental.pallas import tpu as pltpu
from jax.sharding import PartitionSpec as P

negative_fill = -1e30
ROWS = 256


def dot_nt(a, b):
    return lax.dot_general(a, b, (((1,), (1,)), ((), ())), preferred_element_type=jnp.float32)


def attend_kernel(place_ref, q_ref, start_ref, gathered_ref, out_ref, lse_ref, vals_ref, starts_ref):
    span, head_dim = q_ref.shape
    shard = gathered_ref.shape[3] // 2
    pos, core = place_ref[0], place_ref[1]
    scale = 1.0 / math.sqrt(head_dim)
    to_log2 = scale * math.log2(math.e)
    where = ((core, 0), (1 - core, 1 - core), (core, 1))
    for i, (c, j) in enumerate(where):
        vals_ref[i, :, :head_dim] = gathered_ref[c, :, j, shard:, :].reshape(span, head_dim)
    vals_ref[:, :, head_dim:] = jnp.ones((3, span, head_dim), vals_ref.dtype)
    starts_ref[...] = jnp.broadcast_to(start_ref[...], (head_dim, span)).T
    keys = [gathered_ref[c, :, j, :shard, :].reshape(span, head_dim) for c, j in where]

    for r in range(span // ROWS):
        rows = slice(r * ROWS, (r + 1) * ROWS)
        q = q_ref[rows, :]
        starts = starts_ref[rows, :1]
        query_pos = pos * span + r * ROWS + lax.broadcasted_iota(jnp.int32, (ROWS, 1), 0)
        parts = []
        for i in range(3):
            width = (r + 1) * ROWS if i == 0 else span
            scores = dot_nt(q, keys[i][:width])
            key_pos = (pos - i) * span + lax.broadcasted_iota(jnp.int32, (ROWS, width), 1)
            visible = key_pos >= starts
            if i == 0:
                visible &= key_pos <= query_pos
            parts.append(jnp.where(visible, scores, negative_fill))
        top = functools.reduce(jnp.maximum, [jnp.max(s, axis=1, keepdims=True) for s in parts])
        total = 0.0
        for i, s in enumerate(parts):
            weights = jnp.exp2((s - top) * to_log2).astype(jnp.bfloat16)
            total += jnp.dot(weights, vals_ref[i, : s.shape[1]], preferred_element_type=jnp.float32)
        sums = total[:, head_dim:]
        out_ref[rows, :] = (total[:, :head_dim] / sums).astype(out_ref.dtype)
        lse_ref[:, rows] = (top * scale + jnp.log(sums)).T[:1]


def attend(place, queries, doc_start, gathered):
    span, head_dim = queries.shape
    vmem = pl.BlockSpec(memory_space=pltpu.VMEM)
    return pl.pallas_call(
        attend_kernel,
        out_shape=(
            jax.ShapeDtypeStruct((span, head_dim), jnp.bfloat16),
            jax.ShapeDtypeStruct((1, span), jnp.float32),
        ),
        in_specs=[pl.BlockSpec(memory_space=pltpu.SMEM), vmem, vmem, vmem],
        out_specs=(vmem, vmem),
        scratch_shapes=[
            pltpu.VMEM((3, span, 2 * head_dim), jnp.bfloat16),
            pltpu.VMEM((span, head_dim), jnp.int32),
        ],
        compiler_params=pltpu.CompilerParams(vmem_limit_bytes=32 * 1024 * 1024),
    )(place, queries, doc_start, gathered)


def body(queries, keys, values, doc_start):
    span = doc_start.shape[0]
    pos = lax.axis_index("seq")
    count, heads = lax.axis_size("seq"), lax.axis_size("head")
    own = jnp.concatenate([keys, values], axis=0)
    shifted = lax.ppermute(own, "seq", [(i, i + 2) for i in range(count - 2)])
    pair = jnp.stack([own, shifted])
    block = lax.all_to_all(jnp.broadcast_to(pair[None], (heads,) + pair.shape), "head", 0, 0)
    gathered = lax.all_gather(
        block, "seq", axis=0, axis_index_groups=[[i, i + 1] for i in range(0, count, 2)]
    )
    place = jnp.stack([pos, pos % 2]).astype(jnp.int32)
    return attend(place, queries, doc_start.reshape(1, span), gathered)


def solution(mesh):
    in_specs = (P("seq", "head"), P(("seq", "head"), None), P(("seq", "head"), None), P("seq"))
    out_specs = (P("seq", "head"), P("head", "seq"))
    return jax.shard_map(body, mesh=mesh, in_specs=in_specs, out_specs=out_specs, check_vma=False)
```

time: 116 us -> 93.8 us (0.81)
  the two profiles are of different devices: /device:TPU:2 before, /device:TPU:1 now
where the time goes in v1:
time: 93.8 us; the launch traced here: 93.4 us
  waiting for transfers between devices  47.5 us (51%)
  blocking collectives  18.1 us (19%)
  between operations  14.1 us (15%)
  Pallas kernels  6.36 us (7%)
  starting transfers between devices  3.97 us (4%)
  local copies, waits for them, and re-layouts  3.33 us (4%)
    all_gather x1, waiting for transfers between devices, body(): lax.all_gather(block, 'seq', axis=0, axis_index_groups=[[i, i + 1] for i...  46.2 us
    all_to_all x1, blocking collectives, body(): lax.all_to_all(jnp.broadcast_to(pair[None], (heads,) + pair.shape), 'head...  18.1 us
    pallas_call x1, Pallas kernels, attend(): pl.pallas_call(attend_kernel, out_shape=(jax.ShapeDtypeStruct((span, head...  6.36 us
    ppermute x1, starting transfers between devices, body(): shifted = lax.ppermute(own, 'seq', [(i, i + 2) for i in range(count - 2)])  3.94 us
    unnamed x7, local copies, waits for them, and re-layouts  2.37 us
  transfers between devices with their start and end apart: 2, of which 2 were waited for; matrix products, arithmetic and copies ran while one was open for 0% of the time, Pallas kernels for 0%

profile of v1, /device:TPU:1, one launch (start us, length us, event | category | flops | bytes accessed | tf_op | source)
XLA Modules:
  0.0 93.4 jit_solution(5696648710176022147)
XLA Ops:
  7.2 0.0 all-gather.3.cloned.1.call-start
  7.2 0.8 constant_dynamic-update-slice_fusion.1
  8.0 0.8 constant_dynamic-update-slice_fusion
  8.7 3.9 %collective-permute-start = (bf16[256,128]{1,0:T(8,128)(2,1)S(1)}, bf16[256,128]{1,0:T(8,128)(2,1)S(1)}, u32[]{:S(2)}, u32[]{:S(2)}) collective-permute-start(bf16[256,128]{1,0:T(8,128)(2,1)S(1)} %constant_dynamic-update-slice_fusion), channel_id=1, source_target_pairs={{0,16},{8,24},{16,32},{24,40},{32,48},{40,56},{48,64},{56,72},{64,... | collective-permute-start | bytes 196616 | tf_op jit(solution)/shard_map/ppermute | solution.py:80
  12.7 1.3 %collective-permute-done = bf16[256,128]{1,0:T(8,128)(2,1)S(1)} collective-permute-done((bf16[256,128]{1,0:T(8,128)(2,1)S(1)}, bf16[256,128]{1,0:T(8,128)(2,1)S(1)}, u32[]{:S(2)}, u32[]{:S(2)}) %collective-permute-start) | collective-permute-done | bytes 65568 | tf_op jit(solution)/shard_map/ppermute | solution.py:80
  14.0 0.0 copy-start.1
  14.0 0.0 copy-start.2
  14.0 0.2 broadcast_in_dim.2
  14.2 18.1 %all_to_all.5 = bf16[8,2,256,128]{3,2,1,0:T(8,128)(2,1)} all-to-all(bf16[8,2,256,128]{3,2,1,0:T(8,128)(2,1)S(1)} %broadcast_in_dim.2), channel_id=1, replica_groups=mesh['seq'=128,'head'=8] {'head'}, dimensions={0} | all-to-all | bytes 2097152 | tf_op jit(solution)/shard_map/all_to_all | solution.py:82
  32.3 0.0 all-gather.3.cloned.1.call-update
  32.3 0.1 pad_add_fusion.place_ref
  32.4 46.2 %all-gather.3.cloned.1.call-done = bf16[16,2,256,128]{3,2,1,0:T(8,128)(2,1)} async-done(((bf16[8,2,256,128]{3,2,1,0:T(8,128)(2,1)}), bf16[16,2,256,128]{3,2,1,0:T(8,128)(2,1)}) %all-gather.3.cloned.1.call-update) | async-done | bytes 2097168 | tf_op jit(solution)/shard_map/all_gather | solution.py:83
  78.6 0.0 copy-done.1
  78.6 0.0 copy-done.2
  78.6 0.0 copy-start
  78.6 1.6 %copy-done = bf16[16,2,256,128]{3,2,1,0:T(8,128)(2,1)S(1)} copy-done((bf16[16,2,256,128]{3,2,1,0:T(8,128)(2,1)S(1)}, bf16[16,2,256,128]{3,2,1,0:T(8,128)(2,1)}, u32[]{:S(2)}) %copy-start) | copy-done | bytes 2097176
  80.2 6.4 %shard_map.59 = (bf16[1024,128]{1,0:T(8,128)(2,1)}, f32[1,1024]{1,0:T(1,128)}) custom-call(s32[2]{0:T(128)S(1)} %pad_add_fusion.place_ref, bf16[1024,128]{1,0:T(8,128)(2,1)S(1)} %copy-done.1, s32[1,1024]{1,0:T(1,128)S(1)} %bitcast.7, bf16[2,8,2,256,128]{4,3,2,1,0:T(8,128)(2,1)S(1)} %bitcast.6), custom_call_target="tpu_custom_call" | custom-call | tf_op jit(solution)/shard_map/pallas_call | solution.py:59
  (1 shorter events, 0.0 us)
Async XLA Ops:
  7.2 71.5 %all-gather.3.cloned.1.call-start = ((), (), s32[]{:S(2)}) async-start(), calls=%async_computation.1 | async-start | bytes 3145728 | tf_op jit(solution)/shard_map/all_gather | solution.py:83
  8.7 5.3 %collective-permute-start = (bf16[256,128]{1,0:T(8,128)(2,1)S(1)}, bf16[256,128]{1,0:T(8,128)(2,1)S(1)}, u32[]{:S(2)}, u32[]{:S(2)}) collective-permute-start(bf16[256,128]{1,0:T(8,128)(2,1)S(1)} %constant_dynamic-update-slice_fusion), channel_id=1, source_target_pairs={{0,16},{8,24},{16,32},{24,40},{32,48},{40,56},{48,64},{56,72},{64,... | collective-permute-start | bytes 196616 | tf_op jit(solution)/shard_map/ppermute | solution.py:80
  14.0 64.6 %copy-start.1 = (bf16[1024,128]{1,0:T(8,128)(2,1)S(1)}, bf16[1024,128]{1,0:T(8,128)(2,1)}, u32[]{:S(2)}) copy-start(bf16[1024,128]{1,0:T(8,128)(2,1)} %q_ref.1) | copy-start | bytes 786436
  14.0 64.6 %copy-start.2 = (s32[1024]{0:T(1024)S(1)}, s32[1024]{0:T(1024)}, u32[]{:S(2)}) copy-start(s32[1024]{0:T(1024)} %param.7) | copy-start | bytes 12292
  78.6 1.6 %copy-start = (bf16[16,2,256,128]{3,2,1,0:T(8,128)(2,1)S(1)}, bf16[16,2,256,128]{3,2,1,0:T(8,128)(2,1)}, u32[]{:S(2)}) copy-start(bf16[16,2,256,128]{3,2,1,0:T(8,128)(2,1)} %all-gather.3.cloned.1.call-done) | copy-start | bytes 6291460
Sparse Core Ops, SparseCore 0:
  32.4 46.1 all-gather.2

commit v2 on v1

v2 whole, which is shorter than its diff:
```python
import math

import jax
import jax.numpy as jnp
from jax import lax
from jax.experimental import pallas as pl
from jax.experimental.pallas import tpu as pltpu
from jax.sharding import PartitionSpec as P

negative_fill = -1e30
ROWS = 256
VMEM = pl.BlockSpec(memory_space=pltpu.VMEM)
SMEM = pl.BlockSpec(memory_space=pltpu.SMEM)
LN2 = math.log(2.0)


def dot_nt(a, b):
    return lax.dot_general(a, b, (((1,), (1,)), ((), ())), preferred_element_type=jnp.float32)


def scores_of(q, keys, key_base, starts, query_pos):
    rows, width = q.shape[0], keys.shape[0]
    to_log2 = math.log2(math.e) / math.sqrt(q.shape[1])
    key_pos = key_base + lax.broadcasted_iota(jnp.int32, (rows, width), 1)
    visible = key_pos >= starts
    if query_pos is not None:
        visible &= key_pos <= query_pos
    return jnp.where(visible, dot_nt(q, keys) * to_log2, negative_fill)


def weigh(scores, values, top):
    weights = jnp.exp2(scores - top)
    total = jnp.sum(weights, axis=1, keepdims=True)
    mixed = jnp.dot(weights.astype(jnp.bfloat16), values, preferred_element_type=jnp.float32)
    return total, mixed


def block_of(ref, which, kind):
    shards, _, _, shard, head_dim = ref.shape
    return ref[:, which, kind].reshape(shards * shard, head_dim)


def first_kernel(pos_ref, q_ref, start_ref, pair_ref, mixed_ref, log_ref, starts_ref):
    span, head_dim = q_ref.shape
    pos = pos_ref[0]
    starts_ref[...] = jnp.broadcast_to(start_ref[...], (head_dim, span)).T
    own_keys, own_values = block_of(pair_ref, 0, 0), block_of(pair_ref, 0, 1)
    far_keys, far_values = block_of(pair_ref, 1, 0), block_of(pair_ref, 1, 1)
    for r in range(span // ROWS):
        rows, width = slice(r * ROWS, (r + 1) * ROWS), (r + 1) * ROWS
        q, starts = q_ref[rows, :], starts_ref[rows, :1]
        query_pos = pos * span + r * ROWS + lax.broadcasted_iota(jnp.int32, (ROWS, 1), 0)
        own = scores_of(q, own_keys[:width], pos * span, starts, query_pos)
        far = scores_of(q, far_keys, (pos - 2) * span, starts, None)
        top = jnp.maximum(
            jnp.max(own, axis=1, keepdims=True), jnp.max(far, axis=1, keepdims=True)
        )
        own_total, own_mixed = weigh(own, own_values[:width], top)
        far_total, far_mixed = weigh(far, far_values, top)
        total = own_total + far_total
        mixed_ref[rows, :] = (own_mixed + far_mixed) / total
        log_ref[rows, :] = jnp.broadcast_to(top + jnp.log2(total), (ROWS, head_dim))


def second_kernel(pos_ref, q_ref, start_ref, other_ref, mixed_ref, log_ref, out_ref, lse_ref, starts_ref):
    span, head_dim = q_ref.shape
    pos = pos_ref[0]
    which = 1 - lax.rem(pos, 2)
    starts_ref[...] = jnp.broadcast_to(start_ref[...], (head_dim, span)).T
    keys, values = block_of(other_ref, which, 0), block_of(other_ref, which, 1)
    for r in range(span // ROWS):
        rows = slice(r * ROWS, (r + 1) * ROWS)
        scores = scores_of(q_ref[rows, :], keys, (pos - 1) * span, starts_ref[rows, :1], None)
        logs = log_ref[rows, :1]
        top = jnp.maximum(logs, jnp.max(scores, axis=1, keepdims=True))
        before = jnp.exp2(logs - top)
        total, mixed = weigh(scores, values, top)
        total += before
        out_ref[rows, :] = ((mixed_ref[rows, :] * before + mixed) / total).astype(out_ref.dtype)
        lse = (top + jnp.log2(total)) * LN2
        lse_ref[:, rows] = jnp.broadcast_to(lse, (ROWS, head_dim)).T[:1]


def attend_first(pos, queries, starts, pair):
    span, head_dim = queries.shape
    state = jax.ShapeDtypeStruct((span, head_dim), jnp.float32)
    return pl.pallas_call(
        first_kernel,
        out_shape=(state, state),
        in_specs=[SMEM, VMEM, VMEM, VMEM],
        out_specs=(VMEM, VMEM),
        scratch_shapes=[pltpu.VMEM((span, head_dim), jnp.int32)],
        compiler_params=pltpu.CompilerParams(vmem_limit_bytes=32 * 1024 * 1024),
        cost_estimate=pl.CostEstimate(
            flops=4 * span * 2 * span * head_dim, bytes_accessed=3 << 20, transcendentals=2 * span * span
        ),
    )(pos, queries, starts, pair)


def attend_second(pos, queries, starts, other, mixed, logs):
    span, head_dim = queries.shape
    return pl.pallas_call(
        second_kernel,
        out_shape=(
            jax.ShapeDtypeStruct((span, head_dim), jnp.bfloat16),
            jax.ShapeDtypeStruct((1, span), jnp.float32),
        ),
        in_specs=[SMEM, VMEM, VMEM, VMEM, VMEM, VMEM],
        out_specs=(VMEM, VMEM),
        scratch_shapes=[pltpu.VMEM((span, head_dim), jnp.int32)],
        compiler_params=pltpu.CompilerParams(vmem_limit_bytes=32 * 1024 * 1024),
        cost_estimate=pl.CostEstimate(
            flops=4 * span * span * head_dim, bytes_accessed=3 << 20, transcendentals=span * span
        ),
    )(pos, queries, starts, other, mixed, logs)


def stacked(first, second):
    shape = (2,) + first.shape
    at = lax.broadcasted_iota(jnp.int32, shape, 0)
    return jnp.where(at == 0, first[None], second[None])


def body(queries, keys, values, doc_start):
    span = doc_start.shape[0]
    pos = lax.axis_index("seq")
    count, heads = lax.axis_size("seq"), lax.axis_size("head")
    own = stacked(keys, values)
    far = lax.ppermute(own, "seq", [(i, i + 2) for i in range(count - 2)])
    pair = stacked(own, far)
    pair = lax.all_to_all(jnp.broadcast_to(pair[None], (heads,) + pair.shape), "head", 0, 0)
    other = lax.ppermute(pair, "seq", [(i, i ^ 1) for i in range(count)])
    place, starts = jnp.stack([pos]).astype(jnp.int32), doc_start.reshape(1, span)
    mixed, logs = attend_first(place, queries, starts, pair)
    return attend_second(place, queries, starts, other, mixed, logs)


def solution(mesh):
    in_specs = (P("seq", "head"), P(("seq", "head"), None), P(("seq", "head"), None), P("seq"))
    out_specs = (P("seq", "head"), P("head", "seq"))
    return jax.shard_map(body, mesh=mesh, in_specs=in_specs, out_specs=out_specs, check_vma=False)
```

time: 93.8 us -> 45.2 us (0.48)
  waiting for transfers between devices: 47.5 us -> 1.31 us
  between operations: 14.1 us -> 0.7 us
  starting transfers between devices: 3.97 us -> 16 us
  local copies, waits for them, and re-layouts: 3.33 us -> 0.91 us
    all_gather x1 -> x0, waiting for transfers between devices: 46.2 us -> none  [body(): lax.all_gather(block, 'seq', axis=0, axis_index_groups=[[i, i + 1] for i...]
    ppermute x1 -> x2, starting transfers between devices: 3.94 us -> 16 us  [the longest x1 12 us: body(): other = lax.ppermute(pair, 'seq', [(i, i ^ 1) for i in range(count)])]
    unnamed x7 -> x4, local copies, waits for them, and re-layouts: 2.37 us -> 0.68 us
    pallas_call x1 -> x2, Pallas kernels: 6.36 us -> 6.85 us  [the longest x1 3.62 us: attend_first(): pl.pallas_call(first_kernel, out_shape=(state, state), in_specs=[SMEM, VM...]
  transfers between devices with their start and end apart: 2 -> 2, of which waited for: 2 -> 1; matrix products, arithmetic and copies ran while one was open for 0% -> 0% of each run, Pallas kernels for 0% -> 8%
where the time goes in v2:
time: 45.2 us; the launch traced here: 44.8 us
  blocking collectives  18.1 us (40%)
  starting transfers between devices  16 us (35%)
  Pallas kernels  6.85 us (15%)
  waiting for transfers between devices  1.31 us (3%)
  other arithmetic  0.94 us (2%)
  local copies, waits for them, and re-layouts  0.91 us (2%)
  between operations  0.7 us (2%)
    all_to_all x1, blocking collectives, body(): lax.all_to_all(jnp.broadcast_to(pair[None], (heads,) + pair.shape), 'head...  18.1 us
    ppermute x1, starting transfers between devices, body(): other = lax.ppermute(pair, 'seq', [(i, i ^ 1) for i in range(count)])  12 us
    ppermute x1, starting transfers between devices, body(): far = lax.ppermute(own, 'seq', [(i, i + 2) for i in range(count - 2)])  3.94 us
    pallas_call x1, Pallas kernels, attend_first(): pl.pallas_call(first_kernel, out_shape=(state, state), in_specs=[SMEM, VM...  3.62 us
    pallas_call x1, Pallas kernels, attend_second(): pl.pallas_call(second_kernel, out_shape=(jax.ShapeDtypeStruct((span, head...  3.23 us
    ppermute x1, waiting for transfers between devices, body(): far = lax.ppermute(own, 'seq', [(i, i + 2) for i in range(count - 2)])  1.31 us
    select_n x2, other arithmetic, stacked(): return jnp.where(at == 0, first[None], second[None])  0.94 us
  transfers between devices with their start and end apart: 2, of which 1 were waited for; matrix products, arithmetic and copies ran while one was open for 0% of the time, Pallas kernels for 8%

profile of v2, /device:TPU:1, one launch (start us, length us, event | category | flops | bytes accessed | tf_op | source)
XLA Modules:
  0.0 44.8 jit_solution(2612069257954080629)
XLA Ops:
  0.6 0.9 %broadcast_select_fusion.1 = bf16[2,128,128]{2,1,0:T(8,128)(2,1)S(1)} fusion(pred[2]{0:T(512)(128)(4,1)S(1)} %iota_compare_fusion, bf16[128,128]{1,0:T(8,128)(2,1)} %param.6, bf16[128,128]{1,0:T(8,128)(2,1)} %param.5), kind=kLoop, calls=%fused_computation.1 | loop fusion | flops 32768 | bytes 131074 | tf_op jit(solution)/shard_map/jit(_where)/select_n | solution.py:121
  1.5 3.9 %collective-permute-start = (bf16[2,128,128]{2,1,0:T(8,128)(2,1)S(1)}, bf16[2,128,128]{2,1,0:T(8,128)(2,1)S(1)}, u32[]{:S(2)}, u32[]{:S(2)}) collective-permute-start(bf16[2,128,128]{2,1,0:T(8,128)(2,1)S(1)} %broadcast_select_fusion.1), channel_id=1, source_target_pairs={{0,16},{8,24},{16,32},{24,40},{32,48},{40,56},{48,64},{56,72},{64,... | collective-permute-start | bytes 196616 | tf_op jit(solution)/shard_map/ppermute | solution.py:129
  5.4 1.3 %collective-permute-done = bf16[2,128,128]{2,1,0:T(8,128)(2,1)S(1)} collective-permute-done((bf16[2,128,128]{2,1,0:T(8,128)(2,1)S(1)}, bf16[2,128,128]{2,1,0:T(8,128)(2,1)S(1)}, u32[]{:S(2)}, u32[]{:S(2)}) %collective-permute-start) | collective-permute-done | bytes 65568 | tf_op jit(solution)/shard_map/ppermute | solution.py:129
  6.8 0.1 broadcast_select_fusion
  6.8 0.2 broadcast_in_dim.46
  7.1 0.0 copy-start
  7.1 18.1 %all_to_all.5.pair_ref = bf16[8,2,2,128,128]{4,3,2,1,0:T(8,128)(2,1)S(1)} all-to-all(bf16[8,2,2,128,128]{4,3,2,1,0:T(8,128)(2,1)S(1)} %broadcast_in_dim.46), channel_id=1, replica_groups=mesh['seq'=128,'head'=8] {'head'}, dimensions={0} | all-to-all | bytes 2097152 | tf_op jit(solution)/shard_map/all_to_all | solution.py:131
  25.2 12.0 %collective-permute-start.1 = (bf16[8,2,2,128,128]{4,3,2,1,0:T(8,128)(2,1)S(1)}, bf16[8,2,2,128,128]{4,3,2,1,0:T(8,128)(2,1)S(1)}, u32[]{:S(2)}, u32[]{:S(2)}) collective-permute-start(bf16[8,2,2,128,128]{4,3,2,1,0:T(8,128)(2,1)S(1)} %all_to_all.5.pair_ref), channel_id=1, source_target_pairs={{0,8},{8,0},{16,24},{24,16},{32,40},{40,32},{48,56},{56,48},{64,72... | collective-permute-start | bytes 3145736 | tf_op jit(solution)/shard_map/ppermute | solution.py:132
  37.2 0.0 copy-start.1
  37.2 0.0 copy-done
  37.2 0.7 %copy-done.1 = s32[1024]{0:T(1024)S(1)} copy-done((s32[1024]{0:T(1024)S(1)}, s32[1024]{0:T(1024)}, u32[]{:S(2)}) %copy-start.1) | copy-done | bytes 4120
  37.9 3.6 %shard_map.59 = (f32[1024,128]{1,0:T(8,128)S(1)}, f32[1024,128]{1,0:T(8,128)S(1)}) custom-call(s32[1]{0:T(128)} %bitcast.pos_ref, bf16[1024,128]{1,0:T(8,128)(2,1)S(1)} %copy-done, s32[1,1024]{1,0:T(1,128)S(1)} %bitcast.2, bf16[8,2,2,128,128]{4,3,2,1,0:T(8,128)(2,1)S(1)} %all_to_all.5.pair_ref), custom_call_target="tpu_custom_call" | custom-call | flops 1073741824 | bytes 3145728 | tf_op jit(solution)/shard_map/pallas_call | solution.py:87
  41.5 0.0 collective-permute-done.1.other_ref
  41.5 3.2 %shard_map.60 = (bf16[1024,128]{1,0:T(8,128)(2,1)}, f32[1,1024]{1,0:T(1,128)}) custom-call(s32[1]{0:T(128)} %bitcast.pos_ref, bf16[1024,128]{1,0:T(8,128)(2,1)S(1)} %copy-done, s32[1,1024]{1,0:T(1,128)S(1)} %bitcast.3, bf16[8,2,2,128,128]{4,3,2,1,0:T(8,128)(2,1)S(1)} %collective-permute-done.1.other_ref, f32[1024,128]{1,0:T(8,128)S(1)} %get-tuple-element.4.mixed_ref, ...), custom_call_target="tpu_custom_call" | custom-call | flops 536870912 | bytes 3145728 | tf_op jit(solution)/shard_map/pallas_call | solution.py:102
  (1 shorter events, 0.0 us)
Async XLA Ops:
  1.5 5.3 %collective-permute-start = (bf16[2,128,128]{2,1,0:T(8,128)(2,1)S(1)}, bf16[2,128,128]{2,1,0:T(8,128)(2,1)S(1)}, u32[]{:S(2)}, u32[]{:S(2)}) collective-permute-start(bf16[2,128,128]{2,1,0:T(8,128)(2,1)S(1)} %broadcast_select_fusion.1), channel_id=1, source_target_pairs={{0,16},{8,24},{16,32},{24,40},{32,48},{40,56},{48,64},{56,72},{64,... | collective-permute-start | bytes 196616 | tf_op jit(solution)/shard_map/ppermute | solution.py:129
  7.1 30.1 %copy-start = (bf16[1024,128]{1,0:T(8,128)(2,1)S(1)}, bf16[1024,128]{1,0:T(8,128)(2,1)}, u32[]{:S(2)}) copy-start(bf16[1024,128]{1,0:T(8,128)(2,1)} %q_ref.3) | copy-start | bytes 786436
  25.2 16.4 %collective-permute-start.1 = (bf16[8,2,2,128,128]{4,3,2,1,0:T(8,128)(2,1)S(1)}, bf16[8,2,2,128,128]{4,3,2,1,0:T(8,128)(2,1)S(1)}, u32[]{:S(2)}, u32[]{:S(2)}) collective-permute-start(bf16[8,2,2,128,128]{4,3,2,1,0:T(8,128)(2,1)S(1)} %all_to_all.5.pair_ref), channel_id=1, source_target_pairs={{0,8},{8,0},{16,24},{24,16},{32,40},{40,32},{48,56},{56,48},{64,72... | collective-permute-start | bytes 3145736 | tf_op jit(solution)/shard_map/ppermute | solution.py:132
  37.2 0.7 %copy-start.1 = (s32[1024]{0:T(1024)S(1)}, s32[1024]{0:T(1024)}, u32[]{:S(2)}) copy-start(s32[1024]{0:T(1024)} %param.7) | copy-start | bytes 12292

commit v3 on v2

v3 whole, which is shorter than its diff:
```python
import math

import jax
import jax.numpy as jnp
from jax import lax
from jax.experimental import pallas as pl
from jax.experimental.pallas import tpu as pltpu
from jax.sharding import PartitionSpec as P

negative_fill = -1e30
ROWS = 256
VMEM = pl.BlockSpec(memory_space=pltpu.VMEM)
SMEM = pl.BlockSpec(memory_space=pltpu.SMEM)
HBM = pl.BlockSpec(memory_space=pltpu.HBM)
LN2 = math.log(2.0)
VMEM_LIMIT = 32 * 1024 * 1024
AXES = ("seq", "head")


def dot_nt(a, b):
    return lax.dot_general(a, b, (((1,), (1,)), ((), ())), preferred_element_type=jnp.float32)


def hide(products, key_base, starts, query_pos=None):
    to_log2 = math.log2(math.e) / math.sqrt(128)
    key_pos = key_base + lax.broadcasted_iota(jnp.int32, products.shape, 1)
    visible = key_pos >= starts
    if query_pos is not None:
        visible &= key_pos <= query_pos
    return jnp.where(visible, products * to_log2, negative_fill)


def top_of(scores):
    return jnp.max(scores, axis=1, keepdims=True)


def weigh(scores, values, top):
    weights = jnp.exp2(scores - top)
    total = jnp.sum(weights, axis=1, keepdims=True)
    mixed = jnp.dot(weights.astype(jnp.bfloat16), values, preferred_element_type=jnp.float32)
    return total, mixed


def block_of(ref, side, kind):
    rows = ref.shape[0] * ref.shape[2] * ref.shape[4]
    return ref[:, side, :, kind].reshape(rows, ref.shape[5])


def first_kernel(pos_ref, q_ref, start_ref, held_ref, mixed_ref, log_ref, starts_ref, row_ref, sem):
    span, head_dim = q_ref.shape
    pos = pos_ref[0]
    side = lax.rem(pos // 2, 2)
    fetch = pltpu.make_async_copy(start_ref, row_ref, sem)
    fetch.start()
    own_keys, own_values = block_of(held_ref, side, 0), block_of(held_ref, side, 1)
    far_keys, far_values = block_of(held_ref, 1 - side, 0), block_of(held_ref, 1 - side, 1)

    def products_of(r):
        rows = slice(r * ROWS, (r + 1) * ROWS)
        q = q_ref[rows, :]
        past = dot_nt(q, own_keys[: r * ROWS]) if r else None
        return dot_nt(q, own_keys[rows]), past, dot_nt(q, far_keys)

    upcoming = products_of(0)
    fetch.wait()
    starts_ref[...] = jnp.broadcast_to(row_ref[...], (head_dim, span)).T
    for r in range(span // ROWS):
        rows = slice(r * ROWS, (r + 1) * ROWS)
        near, past, far = upcoming
        if (r + 1) * ROWS < span:
            upcoming = products_of(r + 1)
        starts = starts_ref[rows, :1]
        query_pos = pos * span + r * ROWS + lax.broadcasted_iota(jnp.int32, (ROWS, 1), 0)
        parts = [
            (hide(near, pos * span + r * ROWS, starts, query_pos), own_values[rows]),
            (hide(far, (pos - 2) * span, starts), far_values),
        ]
        if r:
            parts.append((hide(past, pos * span, starts), own_values[: r * ROWS]))
        top = top_of(parts[0][0])
        for scores, _ in parts[1:]:
            top = jnp.maximum(top, top_of(scores))
        total, mixed = 0.0, 0.0
        for scores, values in parts:
            part_total, part_mixed = weigh(scores, values, top)
            total += part_total
            mixed += part_mixed
        mixed_ref[rows, :] = mixed / total
        log_ref[rows, :] = jnp.broadcast_to(top + jnp.log2(total), (ROWS, head_dim))


def second_kernel(pos_ref, q_ref, starts_ref, other_ref, mixed_ref, log_ref, out_ref, lse_ref, out_vmem, lse_vmem, sems):
    span, head_dim = q_ref.shape
    pos = pos_ref[0]
    side, odd = lax.rem(pos // 2, 2), lax.rem(pos, 2)
    side = jnp.where(odd == 1, side, 1 - side)
    keys, values = block_of(other_ref, side, 0), block_of(other_ref, side, 1)
    sends = []
    for r in range(span // ROWS):
        rows = slice(r * ROWS, (r + 1) * ROWS)
        scores = hide(dot_nt(q_ref[rows, :], keys), (pos - 1) * span, starts_ref[rows, :1])
        logs = log_ref[rows, :1]
        top = jnp.maximum(logs, top_of(scores))
        before = jnp.exp2(logs - top)
        total, mixed = weigh(scores, values, top)
        total += before
        out_vmem[rows, :] = ((mixed_ref[rows, :] * before + mixed) / total).astype(out_ref.dtype)
        sends.append(pltpu.make_async_copy(out_vmem.at[rows], out_ref.at[rows], sems.at[r]))
        sends[-1].start()
        lse = (top + jnp.log2(total)) * LN2
        lse_vmem[:, rows] = jnp.broadcast_to(lse, (ROWS, head_dim)).T[:1]
    sends.append(pltpu.make_async_copy(lse_vmem, lse_ref, sems.at[span // ROWS]))
    sends[-1].start()
    for send in sends:
        send.wait()


def attend(pos, queries, doc_start, held, other):
    span, head_dim = queries.shape
    state = jax.ShapeDtypeStruct((span, head_dim), jnp.float32)
    params = pltpu.CompilerParams(vmem_limit_bytes=VMEM_LIMIT)

    def cost(blocks):
        return pl.CostEstimate(
            flops=4 * blocks * span * span * head_dim,
            bytes_accessed=3 << 20,
            transcendentals=blocks * span * span,
        )

    mixed, logs, starts = pl.pallas_call(
        first_kernel,
        out_shape=(state, state, jax.ShapeDtypeStruct((span, head_dim), jnp.int32)),
        in_specs=[SMEM, VMEM, HBM, VMEM],
        out_specs=(VMEM, VMEM, VMEM),
        scratch_shapes=[pltpu.VMEM((1, span), jnp.int32), pltpu.SemaphoreType.DMA],
        compiler_params=params,
        cost_estimate=cost(2),
    )(pos, queries, doc_start.reshape(1, span), held)
    return pl.pallas_call(
        second_kernel,
        out_shape=(
            jax.ShapeDtypeStruct((span, head_dim), jnp.bfloat16),
            jax.ShapeDtypeStruct((1, span), jnp.float32),
        ),
        in_specs=[SMEM, VMEM, VMEM, VMEM, VMEM, VMEM],
        out_specs=(HBM, HBM),
        scratch_shapes=[
            pltpu.VMEM((span, head_dim), jnp.bfloat16),
            pltpu.VMEM((1, span), jnp.float32),
            pltpu.SemaphoreType.DMA((span // ROWS + 1,)),
        ],
        compiler_params=params,
        cost_estimate=cost(1),
    )(pos, queries, starts, other, mixed, logs)


def body(queries, keys, values, doc_start):
    span, (shard, head_dim) = doc_start.shape[0], keys.shape
    count, heads = lax.axis_size("seq"), lax.axis_size("head")
    pos = lax.axis_index("seq")
    width = heads // 2
    own = jnp.where(lax.broadcasted_iota(jnp.int32, (2, shard, head_dim), 0) == 0, keys[None], values[None])
    upward = [(i, i + 4) for i in range(count - 4) if i % 4 >= 2]
    below = lax.ppermute(own, "seq", upward)
    to_side = lax.broadcasted_iota(jnp.int32, (2, 2, width) + own.shape, 1)
    sent = jnp.where((to_side == 0) & (pos % 4 >= 2), below, own)
    slabs = [
        [(z * 4 + side * 2 + core) * heads + high * width + y for high in range(2) for side in range(2) for y in range(width)]
        for z in range(count // 4)
        for core in range(2)
    ]
    held = lax.all_to_all(sent.reshape((4 * width,) + own.shape), AXES, 0, 0, axis_index_groups=slabs)
    held = held.reshape(sent.shape)
    other = lax.ppermute(held, "seq", [(i, i ^ 1) for i in range(count)])
    return attend(jnp.stack([pos]).astype(jnp.int32), queries, doc_start, held, other)


def solution(mesh):
    in_specs = (P("seq", "head"), P(("seq", "head"), None), P(("seq", "head"), None), P("seq"))
    out_specs = (P("seq", "head"), P("head", "seq"))
    return jax.shard_map(body, mesh=mesh, in_specs=in_specs, out_specs=out_specs, check_vma=False)
```

time: 45.2 us -> 41.3 us (0.914)
  starting transfers between devices: 16 us -> 9.42 us
  blocking collectives: 18.1 us -> 23.1 us
  waiting for transfers between devices: 1.31 us -> 0.01 us
  local copies, waits for them, and re-layouts: 0.91 us -> 0.17 us
    ppermute x2, starting transfers between devices: 16 us -> 9.42 us  [the longest x1 8.77 us: body(): other = lax.ppermute(held, 'seq', [(i, i ^ 1) for i in range(count)])]
    all_to_all x1, blocking collectives: 18.1 us -> 23.1 us  [body(): lax.all_to_all(sent.reshape((4 * width,) + own.shape), AXES, 0, 0, axis_i...]
    ppermute x2, waiting for transfers between devices: 1.31 us -> 0.01 us  [the longest x1 0.01 us: body(): below = lax.ppermute(own, 'seq', upward)]
    unnamed x4, local copies, waits for them, and re-layouts: 0.68 us -> 0.01 us
  transfers between devices with their start and end apart: 2 -> 2, of which waited for: 1 -> 0; matrix products, arithmetic and copies ran while one was open for 0% -> 0% of each run, Pallas kernels for 8% -> 8%
where the time goes in v3:
time: 41.3 us; the launch traced here: 40.9 us
  blocking collectives  23.1 us (56%)
  starting transfers between devices  9.42 us (23%)
  Pallas kernels  6.53 us (16%)
  other arithmetic  1.01 us (2%)
  between operations  0.72 us (2%)
    all_to_all x1, blocking collectives, body(): lax.all_to_all(sent.reshape((4 * width,) + own.shape), AXES, 0, 0, axis_i...  23.1 us
    ppermute x1, starting transfers between devices, body(): other = lax.ppermute(held, 'seq', [(i, i ^ 1) for i in range(count)])  8.77 us
    pallas_call x1, Pallas kernels, attend(): pl.pallas_call(first_kernel, out_shape=(state, state, jax.ShapeDtypeStruc...  3.47 us
    pallas_call x1, Pallas kernels, attend(): pl.pallas_call(second_kernel, out_shape=(jax.ShapeDtypeStruct((span, head...  3.07 us
    select_n x1, other arithmetic, body(): jnp.where(lax.broadcasted_iota(jnp.int32, (2, shard, head_dim), 0) == 0,...  0.86 us
  transfers between devices with their start and end apart: 2, of which 0 were waited for; matrix products, arithmetic and copies ran while one was open for 0% of the time, Pallas kernels for 8%

profile of v3, /device:TPU:1, one launch (start us, length us, event | category | flops | bytes accessed | tf_op | source)
XLA Modules:
  0.0 40.9 jit_solution(5918548551289999027)
XLA Ops:
  0.6 0.9 %broadcast_select_fusion.1 = bf16[2,128,128]{2,1,0:T(8,128)(2,1)S(1)} fusion(pred[2]{0:T(512)(128)(4,1)S(1)} %iota_compare_fusion, bf16[128,128]{1,0:T(8,128)(2,1)} %param.6, bf16[128,128]{1,0:T(8,128)(2,1)} %param.5), kind=kLoop, calls=%fused_computation.1 | loop fusion | flops 32768 | bytes 131074 | tf_op jit(solution)/shard_map/jit(_where)/select_n | solution.py:162
  1.5 0.7 %collective-permute-start = (bf16[2,128,128]{2,1,0:T(8,128)(2,1)S(1)}, bf16[2,128,128]{2,1,0:T(8,128)(2,1)S(1)}, u32[]{:S(2)}, u32[]{:S(2)}) collective-permute-start(bf16[2,128,128]{2,1,0:T(8,128)(2,1)S(1)} %broadcast_select_fusion.1), channel_id=1, source_target_pairs={{16,48},{24,56},{48,80},{56,88},{80,112},{88,120},{112,144},{120,1... | collective-permute-start | bytes 196616 | tf_op jit(solution)/shard_map/ppermute | solution.py:164
  2.2 0.1 iota.15
  2.3 0.1 and.21
  2.3 0.0 collective-permute-done
  2.4 0.1 broadcast_select_fusion
  2.5 0.0 copy-start
  2.5 23.1 %all_to_all.5 = bf16[16,2,128,128]{3,2,1,0:T(8,128)(2,1)S(1)} all-to-all(bf16[16,2,128,128]{3,2,1,0:T(8,128)(2,1)S(1)} %broadcast_select_fusion), channel_id=1, replica_groups={{0,1,2,3,16,17,18,19,4,5,6,7,20,21,22,23},{8,9,10,11,24,25,26,27,12,13,..., dimensions={0} | all-to-all | bytes 2097152 | tf_op jit(solution)/shard_map/all_to_all | solution.py:172
  25.6 0.0 copy-start.1
  25.6 8.8 %collective-permute-start.1 = (bf16[2,2,4,2,128,128]{5,4,3,2,1,0:T(8,128)(2,1)S(1)}, bf16[2,2,4,2,128,128]{5,4,3,2,1,0:T(8,128)(2,1)S(1)}, u32[]{:S(2)}, u32[]{:S(2)}) collective-permute-start(bf16[2,2,4,2,128,128]{5,4,3,2,1,0:T(8,128)(2,1)S(1)} %bitcast.3), channel_id=1, source_target_pairs={{0,8},{8,0},{16,24},{24,16},{32,40},{40,32},{48,56},{56,48},{64,72... | collective-permute-start | bytes 3145736 | tf_op jit(solution)/shard_map/ppermute | solution.py:174
  34.4 0.0 copy-done
  34.4 0.0 copy-done.1
  34.4 3.5 %shard_map.59 = (f32[1024,128]{1,0:T(8,128)S(1)}, f32[1024,128]{1,0:T(8,128)S(1)}, s32[1024,128]{1,0:T(8,128)S(1)}) custom-call(s32[1]{0:T(128)} %bitcast.pos_ref, bf16[1024,128]{1,0:T(8,128)(2,1)S(1)} %copy-done, s32[1,1024]{1,0:T(1,128)S(1)} %bitcast.5, bf16[2,2,4,2,128,128]{5,4,3,2,1,0:T(8,128)(2,1)S(1)} %bitcast.4), custom_call_target="tpu_custom_call" | custom-call | flops 1073741824 | bytes 3145728 | tf_op jit(solution)/shard_map/pallas_call | solution.py:130
  37.9 0.0 collective-permute-done.1.other_ref
  37.9 3.1 %shard_map.60 = (bf16[1024,128]{1,0:T(8,128)(2,1)}, f32[1,1024]{1,0:T(1,128)}) custom-call(s32[1]{0:T(128)} %bitcast.pos_ref, bf16[1024,128]{1,0:T(8,128)(2,1)S(1)} %copy-done, s32[1024,128]{1,0:T(8,128)S(1)} %get-tuple-element.5.starts_ref, bf16[2,2,4,2,128,128]{5,4,3,2,1,0:T(8,128)(2,1)S(1)} %collective-permute-done.1.other_ref, ...), custom_call_target="tpu_custom_call" | custom-call | flops 536870912 | bytes 3145728 | tf_op jit(solution)/shard_map/pallas_call | solution.py:139
  (2 shorter events, 0.0 us)
Async XLA Ops:
  1.5 0.9 %collective-permute-start = (bf16[2,128,128]{2,1,0:T(8,128)(2,1)S(1)}, bf16[2,128,128]{2,1,0:T(8,128)(2,1)S(1)}, u32[]{:S(2)}, u32[]{:S(2)}) collective-permute-start(bf16[2,128,128]{2,1,0:T(8,128)(2,1)S(1)} %broadcast_select_fusion.1), channel_id=1, source_target_pairs={{16,48},{24,56},{48,80},{56,88},{80,112},{88,120},{112,144},{120,1... | collective-permute-start | bytes 196616 | tf_op jit(solution)/shard_map/ppermute | solution.py:164
  2.5 31.9 %copy-start = (bf16[1024,128]{1,0:T(8,128)(2,1)S(1)}, bf16[1024,128]{1,0:T(8,128)(2,1)}, u32[]{:S(2)}) copy-start(bf16[1024,128]{1,0:T(8,128)(2,1)} %q_ref.3) | copy-start | bytes 786436
  25.6 8.8 %copy-start.1 = (s32[1024]{0:T(1024)S(1)}, s32[1024]{0:T(1024)}, u32[]{:S(2)}) copy-start(s32[1024]{0:T(1024)} %param.7) | copy-start | bytes 12292
  25.6 12.3 %collective-permute-start.1 = (bf16[2,2,4,2,128,128]{5,4,3,2,1,0:T(8,128)(2,1)S(1)}, bf16[2,2,4,2,128,128]{5,4,3,2,1,0:T(8,128)(2,1)S(1)}, u32[]{:S(2)}, u32[]{:S(2)}) collective-permute-start(bf16[2,2,4,2,128,128]{5,4,3,2,1,0:T(8,128)(2,1)S(1)} %bitcast.3), channel_id=1, source_target_pairs={{0,8},{8,0},{16,24},{24,16},{32,40},{40,32},{48,56},{56,48},{64,72... | collective-permute-start | bytes 3145736 | tf_op jit(solution)/shard_map/ppermute | solution.py:174

commit v4 on v3

--- a/solution.py
+++ b/solution.py
@@ -35,10 +35,14 @@
 
 
 def weigh(scores, values, top):
-    weights = jnp.exp2(scores - top)
-    total = jnp.sum(weights, axis=1, keepdims=True)
-    mixed = jnp.dot(weights.astype(jnp.bfloat16), values, preferred_element_type=jnp.float32)
-    return total, mixed
+    weights = jnp.exp2(scores - top).astype(jnp.bfloat16)
+    return jnp.dot(weights, values, preferred_element_type=jnp.float32)
+
+
+def beside_ones(values, both_ref):
+    head_dim = values.shape[1]
+    both_ref[:, :head_dim] = values
+    both_ref[:, head_dim:] = jnp.ones_like(values)
 
 
 def block_of(ref, side, kind):
@@ -46,14 +50,13 @@
     return ref[:, side, :, kind].reshape(rows, ref.shape[5])
 
 
-def first_kernel(pos_ref, q_ref, start_ref, held_ref, mixed_ref, log_ref, starts_ref, row_ref, sem):
+def first_kernel(pos_ref, q_ref, start_ref, held_ref, mixed_ref, log_ref, starts_ref, row_ref, own_ref, far_ref, sem):
     span, head_dim = q_ref.shape
     pos = pos_ref[0]
     side = lax.rem(pos // 2, 2)
     fetch = pltpu.make_async_copy(start_ref, row_ref, sem)
     fetch.start()
-    own_keys, own_values = block_of(held_ref, side, 0), block_of(held_ref, side, 1)
-    far_keys, far_values = block_of(held_ref, 1 - side, 0), block_of(held_ref, 1 - side, 1)
+    own_keys, far_keys = block_of(held_ref, side, 0), block_of(held_ref, 1 - side, 0)
 
     def products_of(r):
         rows = slice(r * ROWS, (r + 1) * ROWS)
@@ -62,6 +65,8 @@
         return dot_nt(q, own_keys[rows]), past, dot_nt(q, far_keys)
 
     upcoming = products_of(0)
+    beside_ones(block_of(held_ref, side, 1), own_ref)
+    beside_ones(block_of(held_ref, 1 - side, 1), far_ref)
     fetch.wait()
     starts_ref[...] = jnp.broadcast_to(row_ref[...], (head_dim, span)).T
     for r in range(span // ROWS):
@@ -72,53 +77,65 @@
         starts = starts_ref[rows, :1]
         query_pos = pos * span + r * ROWS + lax.broadcasted_iota(jnp.int32, (ROWS, 1), 0)
         parts = [
-            (hide(near, pos * span + r * ROWS, starts, query_pos), own_values[rows]),
-            (hide(far, (pos - 2) * span, starts), far_values),
+            (hide(near, pos * span + r * ROWS, starts, query_pos), own_ref[rows, :]),
+            (hide(far, (pos - 2) * span, starts), far_ref[...]),
         ]
         if r:
-            parts.append((hide(past, pos * span, starts), own_values[: r * ROWS]))
+            parts.append((hide(past, pos * span, starts), own_ref[: r * ROWS, :]))
         top = top_of(parts[0][0])
         for scores, _ in parts[1:]:
             top = jnp.maximum(top, top_of(scores))
-        total, mixed = 0.0, 0.0
-        for scores, values in parts:
-            part_total, part_mixed = weigh(scores, values, top)
-            total += part_total
-            mixed += part_mixed
-        mixed_ref[rows, :] = mixed / total
-        log_ref[rows, :] = jnp.broadcast_to(top + jnp.log2(total), (ROWS, head_dim))
+        sums = sum(weigh(scores, values, top) for scores, values in parts)
+        total = sums[:, head_dim:]
+        mixed_ref[rows, :] = sums[:, :head_dim] / total
+        log_ref[rows, :] = top + jnp.log2(total)
 
 
-def second_kernel(pos_ref, q_ref, starts_ref, other_ref, mixed_ref, log_ref, out_ref, lse_ref, out_vmem, lse_vmem, sems):
+def second_kernel(pos_ref, q_ref, starts_ref, other_ref, mixed_ref, log_ref, out_ref, lse_ref, both_ref, out_vmem, lse_vmem, sems):
     span, head_dim = q_ref.shape
     pos = pos_ref[0]
     side, odd = lax.rem(pos // 2, 2), lax.rem(pos, 2)
     side = jnp.where(odd == 1, side, 1 - side)
-    keys, values = block_of(other_ref, side, 0), block_of(other_ref, side, 1)
+    keys = block_of(other_ref, side, 0)
+    products = [dot_nt(q_ref[:ROWS, :], keys)]
+    beside_ones(block_of(other_ref, side, 1), both_ref)
     sends = []
     for r in range(span // ROWS):
         rows = slice(r * ROWS, (r + 1) * ROWS)
-        scores = hide(dot_nt(q_ref[rows, :], keys), (pos - 1) * span, starts_ref[rows, :1])
-        logs = log_ref[rows, :1]
-        top = jnp.maximum(logs, top_of(scores))
-        before = jnp.exp2(logs - top)
-        total, mixed = weigh(scores, values, top)
-        total += before
-        out_vmem[rows, :] = ((mixed_ref[rows, :] * before + mixed) / total).astype(out_ref.dtype)
+        scores = hide(products.pop(0), (pos - 1) * span, starts_ref[rows, :1])
+        if (r + 1) * ROWS < span:
+            products.append(dot_nt(q_ref[(r + 1) * ROWS : (r + 2) * ROWS, :], keys))
+        top = top_of(scores)
+        sums = weigh(scores, both_ref[...], top)
+        logs = log_ref[rows, :]
+        joint = jnp.maximum(logs, top)
+        before, after = jnp.exp2(logs - joint), jnp.exp2(top - joint)
+        total = sums[:, head_dim:] * after + before
+        mixed = mixed_ref[rows, :] * before + sums[:, :head_dim] * after
+        out_vmem[rows, :] = (mixed / total).astype(out_ref.dtype)
         sends.append(pltpu.make_async_copy(out_vmem.at[rows], out_ref.at[rows], sems.at[r]))
         sends[-1].start()
-        lse = (top + jnp.log2(total)) * LN2
-        lse_vmem[:, rows] = jnp.broadcast_to(lse, (ROWS, head_dim)).T[:1]
+        lse_vmem[:, rows] = row_of((joint + jnp.log2(total)) * LN2)
     sends.append(pltpu.make_async_copy(lse_vmem, lse_ref, sems.at[span // ROWS]))
     sends[-1].start()
     for send in sends:
         send.wait()
 
 
+def row_of(column):
+    rows, lanes = column.shape
+    at = lax.broadcasted_iota(jnp.int32, (lanes, lanes), 0) == lax.broadcasted_iota(jnp.int32, (lanes, lanes), 1)
+    picked = [
+        jnp.sum(jnp.where(at, column[i : i + lanes], 0.0), axis=0, keepdims=True) for i in range(0, rows, lanes)
+    ]
+    return jnp.concatenate(picked, axis=1)
+
+
 def attend(pos, queries, doc_start, held, other):
     span, head_dim = queries.shape
     state = jax.ShapeDtypeStruct((span, head_dim), jnp.float32)
     params = pltpu.CompilerParams(vmem_limit_bytes=VMEM_LIMIT)
+    both = pltpu.VMEM((span, 2 * head_dim), jnp.bfloat16)
 
     def cost(blocks):
         return pl.CostEstimate(
@@ -132,7 +149,7 @@
         out_shape=(state, state, jax.ShapeDtypeStruct((span, head_dim), jnp.int32)),
         in_specs=[SMEM, VMEM, HBM, VMEM],
         out_specs=(VMEM, VMEM, VMEM),
-        scratch_shapes=[pltpu.VMEM((1, span), jnp.int32), pltpu.SemaphoreType.DMA],
+        scratch_shapes=[pltpu.VMEM((1, span), jnp.int32), both, both, pltpu.SemaphoreType.DMA],
         compiler_params=params,
         cost_estimate=cost(2),
     )(pos, queries, doc_start.reshape(1, span), held)
@@ -145,6 +162,7 @@
         in_specs=[SMEM, VMEM, VMEM, VMEM, VMEM, VMEM],
         out_specs=(HBM, HBM),
         scratch_shapes=[
+            both,
             pltpu.VMEM((span, head_dim), jnp.bfloat16),
             pltpu.VMEM((1, span), jnp.float32),
             pltpu.SemaphoreType.DMA((span // ROWS + 1,)),

time: 41.3 us -> 40.6 us (0.983)
  Pallas kernels: 6.53 us -> 5.91 us
where the time goes in v4:
time: 40.6 us; the launch traced here: 40.3 us
  blocking collectives  23.1 us (57%)
  starting transfers between devices  9.42 us (23%)
  Pallas kernels  5.91 us (15%)
  other arithmetic  1.01 us (2%)
  between operations  0.72 us (2%)
    all_to_all x1, blocking collectives, body(): lax.all_to_all(sent.reshape((4 * width,) + own.shape), AXES, 0, 0, axis_i...  23.1 us
    ppermute x1, starting transfers between devices, body(): other = lax.ppermute(held, 'seq', [(i, i ^ 1) for i in range(count)])  8.77 us
    pallas_call x1, Pallas kernels, attend(): pl.pallas_call(first_kernel, out_shape=(state, state, jax.ShapeDtypeStruc...  3.22 us
    pallas_call x1, Pallas kernels, attend(): pl.pallas_call(second_kernel, out_shape=(jax.ShapeDtypeStruct((span, head...  2.68 us
    select_n x1, other arithmetic, body(): jnp.where(lax.broadcasted_iota(jnp.int32, (2, shard, head_dim), 0) == 0,...  0.86 us
  transfers between devices with their start and end apart: 2, of which 0 were waited for; matrix products, arithmetic and copies ran while one was open for 0% of the time, Pallas kernels for 8%

profile of v4, /device:TPU:1, one launch (start us, length us, event | category | flops | bytes accessed | tf_op | source)
XLA Modules:
  0.0 40.3 jit_solution(9763321090334423837)
XLA Ops:
  0.6 0.9 %broadcast_select_fusion.1 = bf16[2,128,128]{2,1,0:T(8,128)(2,1)S(1)} fusion(pred[2]{0:T(512)(128)(4,1)S(1)} %iota_compare_fusion, bf16[128,128]{1,0:T(8,128)(2,1)} %param.6, bf16[128,128]{1,0:T(8,128)(2,1)} %param.5), kind=kLoop, calls=%fused_computation.1 | loop fusion | flops 32768 | bytes 131074 | tf_op jit(solution)/shard_map/jit(_where)/select_n | solution.py:180
  1.5 0.7 %collective-permute-start = (bf16[2,128,128]{2,1,0:T(8,128)(2,1)S(1)}, bf16[2,128,128]{2,1,0:T(8,128)(2,1)S(1)}, u32[]{:S(2)}, u32[]{:S(2)}) collective-permute-start(bf16[2,128,128]{2,1,0:T(8,128)(2,1)S(1)} %broadcast_select_fusion.1), channel_id=1, source_target_pairs={{16,48},{24,56},{48,80},{56,88},{80,112},{88,120},{112,144},{120,1... | collective-permute-start | bytes 196616 | tf_op jit(solution)/shard_map/ppermute | solution.py:182
  2.2 0.1 iota.15
  2.3 0.1 and.21
  2.3 0.0 collective-permute-done
  2.4 0.1 broadcast_select_fusion
  2.5 0.0 copy-start
  2.5 23.1 %all_to_all.5 = bf16[16,2,128,128]{3,2,1,0:T(8,128)(2,1)S(1)} all-to-all(bf16[16,2,128,128]{3,2,1,0:T(8,128)(2,1)S(1)} %broadcast_select_fusion), channel_id=1, replica_groups={{0,1,2,3,16,17,18,19,4,5,6,7,20,21,22,23},{8,9,10,11,24,25,26,27,12,13,..., dimensions={0} | all-to-all | bytes 2097152 | tf_op jit(solution)/shard_map/all_to_all | solution.py:190
  25.6 0.0 copy-start.1
  25.6 8.8 %collective-permute-start.1 = (bf16[2,2,4,2,128,128]{5,4,3,2,1,0:T(8,128)(2,1)S(1)}, bf16[2,2,4,2,128,128]{5,4,3,2,1,0:T(8,128)(2,1)S(1)}, u32[]{:S(2)}, u32[]{:S(2)}) collective-permute-start(bf16[2,2,4,2,128,128]{5,4,3,2,1,0:T(8,128)(2,1)S(1)} %bitcast.3), channel_id=1, source_target_pairs={{0,8},{8,0},{16,24},{24,16},{32,40},{40,32},{48,56},{56,48},{64,72... | collective-permute-start | bytes 3145736 | tf_op jit(solution)/shard_map/ppermute | solution.py:192
  34.4 0.0 copy-done
  34.4 0.0 copy-done.1
  34.4 3.2 %shard_map.59 = (f32[1024,128]{1,0:T(8,128)S(1)}, f32[1024,128]{1,0:T(8,128)S(1)}, s32[1024,128]{1,0:T(8,128)S(1)}) custom-call(s32[1]{0:T(128)} %bitcast.pos_ref, bf16[1024,128]{1,0:T(8,128)(2,1)S(1)} %copy-done, s32[1,1024]{1,0:T(1,128)S(1)} %bitcast.5, bf16[2,2,4,2,128,128]{5,4,3,2,1,0:T(8,128)(2,1)S(1)} %bitcast.4), custom_call_target="tpu_custom_call" | custom-call | flops 1073741824 | bytes 3145728 | tf_op jit(solution)/shard_map/pallas_call | solution.py:147
  37.6 0.0 collective-permute-done.1.other_ref
  37.6 2.7 %shard_map.60 = (bf16[1024,128]{1,0:T(8,128)(2,1)}, f32[1,1024]{1,0:T(1,128)}) custom-call(s32[1]{0:T(128)} %bitcast.pos_ref, bf16[1024,128]{1,0:T(8,128)(2,1)S(1)} %copy-done, s32[1024,128]{1,0:T(8,128)S(1)} %get-tuple-element.5.starts_ref, bf16[2,2,4,2,128,128]{5,4,3,2,1,0:T(8,128)(2,1)S(1)} %collective-permute-done.1.other_ref, ...), custom_call_target="tpu_custom_call" | custom-call | flops 536870912 | bytes 3145728 | tf_op jit(solution)/shard_map/pallas_call | solution.py:156
  (2 shorter events, 0.0 us)
Async XLA Ops:
  1.5 0.9 %collective-permute-start = (bf16[2,128,128]{2,1,0:T(8,128)(2,1)S(1)}, bf16[2,128,128]{2,1,0:T(8,128)(2,1)S(1)}, u32[]{:S(2)}, u32[]{:S(2)}) collective-permute-start(bf16[2,128,128]{2,1,0:T(8,128)(2,1)S(1)} %broadcast_select_fusion.1), channel_id=1, source_target_pairs={{16,48},{24,56},{48,80},{56,88},{80,112},{88,120},{112,144},{120,1... | collective-permute-start | bytes 196616 | tf_op jit(solution)/shard_map/ppermute | solution.py:182
  2.5 31.9 %copy-start = (bf16[1024,128]{1,0:T(8,128)(2,1)S(1)}, bf16[1024,128]{1,0:T(8,128)(2,1)}, u32[]{:S(2)}) copy-start(bf16[1024,128]{1,0:T(8,128)(2,1)} %q_ref.3) | copy-start | bytes 786436
  25.6 8.8 %copy-start.1 = (s32[1024]{0:T(1024)S(1)}, s32[1024]{0:T(1024)}, u32[]{:S(2)}) copy-start(s32[1024]{0:T(1024)} %param.7) | copy-start | bytes 12292
  25.6 12.0 %collective-permute-start.1 = (bf16[2,2,4,2,128,128]{5,4,3,2,1,0:T(8,128)(2,1)S(1)}, bf16[2,2,4,2,128,128]{5,4,3,2,1,0:T(8,128)(2,1)S(1)}, u32[]{:S(2)}, u32[]{:S(2)}) collective-permute-start(bf16[2,2,4,2,128,128]{5,4,3,2,1,0:T(8,128)(2,1)S(1)} %bitcast.3), channel_id=1, source_target_pairs={{0,8},{8,0},{16,24},{24,16},{32,40},{40,32},{48,56},{56,48},{64,72... | collective-permute-start | bytes 3145736 | tf_op jit(solution)/shard_map/ppermute | solution.py:192

commit v5 on v4

--- a/solution.py
+++ b/solution.py
@@ -14,6 +14,8 @@
 HBM = pl.BlockSpec(memory_space=pltpu.HBM)
 LN2 = math.log(2.0)
 VMEM_LIMIT = 32 * 1024 * 1024
+HEAD_DIM = 128
+TO_LOG2 = math.log2(math.e) / math.sqrt(HEAD_DIM)
 AXES = ("seq", "head")
 
 
@@ -22,20 +24,22 @@
 
 
 def hide(products, key_base, starts, query_pos=None):
-    to_log2 = math.log2(math.e) / math.sqrt(128)
     key_pos = key_base + lax.broadcasted_iota(jnp.int32, products.shape, 1)
     visible = key_pos >= starts
     if query_pos is not None:
         visible &= key_pos <= query_pos
-    return jnp.where(visible, products * to_log2, negative_fill)
-
-
-def top_of(scores):
-    return jnp.max(scores, axis=1, keepdims=True)
+    return jnp.where(visible, products, negative_fill)
+
+
+def top_of(*parts, lanes=128):
+    pieces = [scores[:, i : i + lanes] for scores in parts for i in range(0, scores.shape[1], lanes)]
+    while len(pieces) > 1:
+        pieces = [jnp.maximum(*pieces[i : i + 2]) if i + 1 < len(pieces) else pieces[i] for i in range(0, len(pieces), 2)]
+    return jnp.max(pieces[0], axis=1, keepdims=True)
 
 
 def weigh(scores, values, top):
-    weights = jnp.exp2(scores - top).astype(jnp.bfloat16)
+    weights = jnp.exp2((scores - top) * TO_LOG2).astype(jnp.bfloat16)
     return jnp.dot(weights, values, preferred_element_type=jnp.float32)
 
 
@@ -82,13 +86,11 @@
         ]
         if r:
             parts.append((hide(past, pos * span, starts), own_ref[: r * ROWS, :]))
-        top = top_of(parts[0][0])
-        for scores, _ in parts[1:]:
-            top = jnp.maximum(top, top_of(scores))
+        top = top_of(*[scores for scores, _ in parts])
         sums = sum(weigh(scores, values, top) for scores, values in parts)
         total = sums[:, head_dim:]
         mixed_ref[rows, :] = sums[:, :head_dim] / total
-        log_ref[rows, :] = top + jnp.log2(total)
+        log_ref[rows, :] = top * TO_LOG2 + jnp.log2(total)
 
 
 def second_kernel(pos_ref, q_ref, starts_ref, other_ref, mixed_ref, log_ref, out_ref, lse_ref, both_ref, out_vmem, lse_vmem, sems):
@@ -107,6 +109,7 @@
             products.append(dot_nt(q_ref[(r + 1) * ROWS : (r + 2) * ROWS, :], keys))
         top = top_of(scores)
         sums = weigh(scores, both_ref[...], top)
+        top = top * TO_LOG2
         logs = log_ref[rows, :]
         joint = jnp.maximum(logs, top)
         before, after = jnp.exp2(logs - joint), jnp.exp2(top - joint)

time: 40.6 us -> 40.2 us (level)
  transfers between devices with their start and end apart: 2 -> 2, of which waited for: 0 -> 0; matrix products, arithmetic and copies ran while one was open for 0% -> 0% of each run, Pallas kernels for 8% -> 7%
where the time goes in v5:
time: 40.2 us; the launch traced here: 39.9 us
  blocking collectives  23.1 us (57%)
  starting transfers between devices  9.42 us (23%)
  Pallas kernels  5.51 us (14%)
  other arithmetic  1.01 us (3%)
  between operations  0.72 us (2%)
    all_to_all x1, blocking collectives, body(): lax.all_to_all(sent.reshape((4 * width,) + own.shape), AXES, 0, 0, axis_i...  23.1 us
    ppermute x1, starting transfers between devices, body(): other = lax.ppermute(held, 'seq', [(i, i ^ 1) for i in range(count)])  8.77 us
    pallas_call x1, Pallas kernels, attend(): pl.pallas_call(first_kernel, out_shape=(state, state, jax.ShapeDtypeStruc...  2.87 us
    pallas_call x1, Pallas kernels, attend(): pl.pallas_call(second_kernel, out_shape=(jax.ShapeDtypeStruct((span, head...  2.63 us
    select_n x1, other arithmetic, body(): jnp.where(lax.broadcasted_iota(jnp.int32, (2, shard, head_dim), 0) == 0,...  0.86 us
  transfers between devices with their start and end apart: 2, of which 0 were waited for; matrix products, arithmetic and copies ran while one was open for 0% of the time, Pallas kernels for 7%

profile of v5, /device:TPU:1, one launch (start us, length us, event | category | flops | bytes accessed | tf_op | source)
XLA Modules:
  0.0 39.9 jit_solution(12392980680612658955)
XLA Ops:
  0.6 0.9 %broadcast_select_fusion.1 = bf16[2,128,128]{2,1,0:T(8,128)(2,1)S(1)} fusion(pred[2]{0:T(512)(128)(4,1)S(1)} %iota_compare_fusion, bf16[128,128]{1,0:T(8,128)(2,1)} %param.6, bf16[128,128]{1,0:T(8,128)(2,1)} %param.5), kind=kLoop, calls=%fused_computation.1 | loop fusion | flops 32768 | bytes 131074 | tf_op jit(solution)/shard_map/jit(_where)/select_n | solution.py:183
  1.5 0.7 %collective-permute-start = (bf16[2,128,128]{2,1,0:T(8,128)(2,1)S(1)}, bf16[2,128,128]{2,1,0:T(8,128)(2,1)S(1)}, u32[]{:S(2)}, u32[]{:S(2)}) collective-permute-start(bf16[2,128,128]{2,1,0:T(8,128)(2,1)S(1)} %broadcast_select_fusion.1), channel_id=1, source_target_pairs={{16,48},{24,56},{48,80},{56,88},{80,112},{88,120},{112,144},{120,1... | collective-permute-start | bytes 196616 | tf_op jit(solution)/shard_map/ppermute | solution.py:185
  2.2 0.1 iota.15
  2.3 0.1 and.21
  2.3 0.0 collective-permute-done
  2.4 0.1 broadcast_select_fusion
  2.5 0.0 copy-start
  2.5 23.1 %all_to_all.5 = bf16[16,2,128,128]{3,2,1,0:T(8,128)(2,1)S(1)} all-to-all(bf16[16,2,128,128]{3,2,1,0:T(8,128)(2,1)S(1)} %broadcast_select_fusion), channel_id=1, replica_groups={{0,1,2,3,16,17,18,19,4,5,6,7,20,21,22,23},{8,9,10,11,24,25,26,27,12,13,..., dimensions={0} | all-to-all | bytes 2097152 | tf_op jit(solution)/shard_map/all_to_all | solution.py:193
  25.6 0.0 copy-start.1
  25.6 8.8 %collective-permute-start.1 = (bf16[2,2,4,2,128,128]{5,4,3,2,1,0:T(8,128)(2,1)S(1)}, bf16[2,2,4,2,128,128]{5,4,3,2,1,0:T(8,128)(2,1)S(1)}, u32[]{:S(2)}, u32[]{:S(2)}) collective-permute-start(bf16[2,2,4,2,128,128]{5,4,3,2,1,0:T(8,128)(2,1)S(1)} %bitcast.3), channel_id=1, source_target_pairs={{0,8},{8,0},{16,24},{24,16},{32,40},{40,32},{48,56},{56,48},{64,72... | collective-permute-start | bytes 3145736 | tf_op jit(solution)/shard_map/ppermute | solution.py:195
  34.4 0.0 copy-done
  34.4 0.0 copy-done.1
  34.4 2.9 %shard_map.59 = (f32[1024,128]{1,0:T(8,128)S(1)}, f32[1024,128]{1,0:T(8,128)S(1)}, s32[1024,128]{1,0:T(8,128)S(1)}) custom-call(s32[1]{0:T(128)} %bitcast.pos_ref, bf16[1024,128]{1,0:T(8,128)(2,1)S(1)} %copy-done, s32[1,1024]{1,0:T(1,128)S(1)} %bitcast.5, bf16[2,2,4,2,128,128]{5,4,3,2,1,0:T(8,128)(2,1)S(1)} %bitcast.4), custom_call_target="tpu_custom_call" | custom-call | flops 1073741824 | bytes 3145728 | tf_op jit(solution)/shard_map/pallas_call | solution.py:150
  37.3 0.0 collective-permute-done.1.other_ref
  37.3 2.6 %shard_map.60 = (bf16[1024,128]{1,0:T(8,128)(2,1)}, f32[1,1024]{1,0:T(1,128)}) custom-call(s32[1]{0:T(128)} %bitcast.pos_ref, bf16[1024,128]{1,0:T(8,128)(2,1)S(1)} %copy-done, s32[1024,128]{1,0:T(8,128)S(1)} %get-tuple-element.5.starts_ref, bf16[2,2,4,2,128,128]{5,4,3,2,1,0:T(8,128)(2,1)S(1)} %collective-permute-done.1.other_ref, ...), custom_call_target="tpu_custom_call" | custom-call | flops 536870912 | bytes 3145728 | tf_op jit(solution)/shard_map/pallas_call | solution.py:159
  (2 shorter events, 0.0 us)
Async XLA Ops:
  1.5 0.9 %collective-permute-start = (bf16[2,128,128]{2,1,0:T(8,128)(2,1)S(1)}, bf16[2,128,128]{2,1,0:T(8,128)(2,1)S(1)}, u32[]{:S(2)}, u32[]{:S(2)}) collective-permute-start(bf16[2,128,128]{2,1,0:T(8,128)(2,1)S(1)} %broadcast_select_fusion.1), channel_id=1, source_target_pairs={{16,48},{24,56},{48,80},{56,88},{80,112},{88,120},{112,144},{120,1... | collective-permute-start | bytes 196616 | tf_op jit(solution)/shard_map/ppermute | solution.py:185
  2.5 31.9 %copy-start = (bf16[1024,128]{1,0:T(8,128)(2,1)S(1)}, bf16[1024,128]{1,0:T(8,128)(2,1)}, u32[]{:S(2)}) copy-start(bf16[1024,128]{1,0:T(8,128)(2,1)} %q_ref.3) | copy-start | bytes 786436
  25.6 8.8 %copy-start.1 = (s32[1024]{0:T(1024)S(1)}, s32[1024]{0:T(1024)}, u32[]{:S(2)}) copy-start(s32[1024]{0:T(1024)} %param.7) | copy-start | bytes 12292
  25.6 11.7 %collective-permute-start.1 = (bf16[2,2,4,2,128,128]{5,4,3,2,1,0:T(8,128)(2,1)S(1)}, bf16[2,2,4,2,128,128]{5,4,3,2,1,0:T(8,128)(2,1)S(1)}, u32[]{:S(2)}, u32[]{:S(2)}) collective-permute-start(bf16[2,2,4,2,128,128]{5,4,3,2,1,0:T(8,128)(2,1)S(1)} %bitcast.3), channel_id=1, source_target_pairs={{0,8},{8,0},{16,24},{24,16},{32,40},{40,32},{48,56},{56,48},{64,72... | collective-permute-start | bytes 3145736 | tf_op jit(solution)/shard_map/ppermute | solution.py:195

commit v6 on v5

--- a/solution.py
+++ b/solution.py
@@ -13,6 +13,7 @@
 SMEM = pl.BlockSpec(memory_space=pltpu.SMEM)
 HBM = pl.BlockSpec(memory_space=pltpu.HBM)
 LN2 = math.log(2.0)
+TOTAL_MAX = 2.0**100
 VMEM_LIMIT = 32 * 1024 * 1024
 HEAD_DIM = 128
 TO_LOG2 = math.log2(math.e) / math.sqrt(HEAD_DIM)
@@ -38,8 +39,9 @@
     return jnp.max(pieces[0], axis=1, keepdims=True)
 
 
-def weigh(scores, values, top):
-    weights = jnp.exp2((scores - top) * TO_LOG2).astype(jnp.bfloat16)
+def weigh(scores, values, shift):
+    wide = jnp.concatenate([shift] * (scores.shape[1] // shift.shape[1]), axis=1) if shift.shape[1] > 1 else shift
+    weights = jnp.exp2(scores * TO_LOG2 - wide).astype(jnp.bfloat16)
     return jnp.dot(weights, values, preferred_element_type=jnp.float32)
 
 
@@ -52,6 +54,27 @@
 def block_of(ref, side, kind):
     rows = ref.shape[0] * ref.shape[2] * ref.shape[4]
     return ref[:, side, :, kind].reshape(rows, ref.shape[5])
+
+
+def query_positions(pos, r, span):
+    return pos * span + r * ROWS + lax.broadcasted_iota(jnp.int32, (ROWS, 1), 0)
+
+
+def products_of(r, q_ref, own_keys, far_keys):
+    rows = slice(r * ROWS, (r + 1) * ROWS)
+    q = q_ref[rows, :]
+    past = dot_nt(q, own_keys[: r * ROWS]) if r else None
+    return dot_nt(q, own_keys[rows]), past, dot_nt(q, far_keys)
+
+
+def parts_of(r, pos, products, starts, own_ref, far_ref):
+    rows, span = slice(r * ROWS, (r + 1) * ROWS), far_ref.shape[0]
+    near, past, far = products
+    parts = [(hide(far, (pos - 2) * span, starts), far_ref[...])]
+    if r:
+        parts.append((hide(past, pos * span, starts), own_ref[: r * ROWS, :]))
+    parts.append((hide(near, pos * span + r * ROWS, starts, query_positions(pos, r, span)), own_ref[rows, :]))
+    return parts
 
 
 def first_kernel(pos_ref, q_ref, start_ref, held_ref, mixed_ref, log_ref, starts_ref, row_ref, own_ref, far_ref, sem):
@@ -61,68 +84,87 @@
     fetch = pltpu.make_async_copy(start_ref, row_ref, sem)
     fetch.start()
     own_keys, far_keys = block_of(held_ref, side, 0), block_of(held_ref, 1 - side, 0)
-
-    def products_of(r):
-        rows = slice(r * ROWS, (r + 1) * ROWS)
-        q = q_ref[rows, :]
-        past = dot_nt(q, own_keys[: r * ROWS]) if r else None
-        return dot_nt(q, own_keys[rows]), past, dot_nt(q, far_keys)
-
-    upcoming = products_of(0)
+    upcoming = products_of(0, q_ref, own_keys, far_keys)
     beside_ones(block_of(held_ref, side, 1), own_ref)
     beside_ones(block_of(held_ref, 1 - side, 1), far_ref)
+    with_own = jnp.sum(q_ref[...].astype(jnp.float32) * own_keys.astype(jnp.float32), axis=1, keepdims=True)
+    log_ref[...] = jnp.broadcast_to(with_own * TO_LOG2, log_ref.shape)
     fetch.wait()
     starts_ref[...] = jnp.broadcast_to(row_ref[...], (head_dim, span)).T
     for r in range(span // ROWS):
         rows = slice(r * ROWS, (r + 1) * ROWS)
-        near, past, far = upcoming
+        products = upcoming
         if (r + 1) * ROWS < span:
-            upcoming = products_of(r + 1)
-        starts = starts_ref[rows, :1]
-        query_pos = pos * span + r * ROWS + lax.broadcasted_iota(jnp.int32, (ROWS, 1), 0)
-        parts = [
-            (hide(near, pos * span + r * ROWS, starts, query_pos), own_ref[rows, :]),
-            (hide(far, (pos - 2) * span, starts), far_ref[...]),
-        ]
-        if r:
-            parts.append((hide(past, pos * span, starts), own_ref[: r * ROWS, :]))
-        top = top_of(*[scores for scores, _ in parts])
-        sums = sum(weigh(scores, values, top) for scores, values in parts)
+            upcoming = products_of(r + 1, q_ref, own_keys, far_keys)
+        shift = log_ref[rows, :]
+        parts = parts_of(r, pos, products, starts_ref[rows, :1], own_ref, far_ref)
+        sums = sum(weigh(scores, values, shift[:, :1]) for scores, values in parts)
         total = sums[:, head_dim:]
         mixed_ref[rows, :] = sums[:, :head_dim] / total
-        log_ref[rows, :] = top * TO_LOG2 + jnp.log2(total)
-
-
-def second_kernel(pos_ref, q_ref, starts_ref, other_ref, mixed_ref, log_ref, out_ref, lse_ref, both_ref, out_vmem, lse_vmem, sems):
+        log_ref[rows, :] = jnp.where(total <= TOTAL_MAX, shift + jnp.log2(total), -jnp.inf)
+
+
+def second_kernel(
+    pos_ref, q_ref, starts_ref, held_ref, other_ref, mixed_ref, log_ref, out_ref, lse_ref, both_ref, own_ref, far_ref, out_vmem, lse_vmem, sems
+):
     span, head_dim = q_ref.shape
     pos = pos_ref[0]
-    side, odd = lax.rem(pos // 2, 2), lax.rem(pos, 2)
-    side = jnp.where(odd == 1, side, 1 - side)
+    own_side, odd = lax.rem(pos // 2, 2), lax.rem(pos, 2)
+    side = jnp.where(odd == 1, own_side, 1 - own_side)
     keys = block_of(other_ref, side, 0)
-    products = [dot_nt(q_ref[:ROWS, :], keys)]
+    tiles = span // ROWS
+
+    def products_with(r):
+        return dot_nt(q_ref[r * ROWS : (r + 1) * ROWS, :], keys)
+
+    def scores_of(r, products):
+        return hide(products, (pos - 1) * span, starts_ref[r * ROWS : (r + 1) * ROWS, :1])
+
+    def send(r):
+        rows = slice(r * ROWS, (r + 1) * ROWS)
+        return pltpu.make_async_copy(out_vmem.at[rows], out_ref.at[rows], sems.at[r])
+
+    send_lse = pltpu.make_async_copy(lse_vmem, lse_ref, sems.at[tiles])
+
+    def finish(r, mixed, total, shift):
+        rows = slice(r * ROWS, (r + 1) * ROWS)
+        out_vmem[rows, :] = (mixed / total).astype(out_ref.dtype)
+        send(r).start()
+        lse_vmem[:, rows] = row_of((shift + jnp.log2(total)) * LN2)
+
+    def end():
+        for r in range(tiles):
+            send(r).wait()
+        send_lse.wait()
+
     beside_ones(block_of(other_ref, side, 1), both_ref)
-    sends = []
-    for r in range(span // ROWS):
-        rows = slice(r * ROWS, (r + 1) * ROWS)
-        scores = hide(products.pop(0), (pos - 1) * span, starts_ref[rows, :1])
-        if (r + 1) * ROWS < span:
-            products.append(dot_nt(q_ref[(r + 1) * ROWS : (r + 2) * ROWS, :], keys))
-        top = top_of(scores)
-        sums = weigh(scores, both_ref[...], top)
-        top = top * TO_LOG2
+    largest = None
+    for r in range(tiles):
+        rows = slice(r * ROWS, (r + 1) * ROWS)
+        products = products_with(r)
         logs = log_ref[rows, :]
-        joint = jnp.maximum(logs, top)
-        before, after = jnp.exp2(logs - joint), jnp.exp2(top - joint)
-        total = sums[:, head_dim:] * after + before
-        mixed = mixed_ref[rows, :] * before + sums[:, :head_dim] * after
-        out_vmem[rows, :] = (mixed / total).astype(out_ref.dtype)
-        sends.append(pltpu.make_async_copy(out_vmem.at[rows], out_ref.at[rows], sems.at[r]))
-        sends[-1].start()
-        lse_vmem[:, rows] = row_of((joint + jnp.log2(total)) * LN2)
-    sends.append(pltpu.make_async_copy(lse_vmem, lse_ref, sems.at[span // ROWS]))
-    sends[-1].start()
-    for send in sends:
-        send.wait()
+        sums = weigh(scores_of(r, products), both_ref[...], logs)
+        total = sums[:, head_dim:] + 1.0
+        finish(r, mixed_ref[rows, :] + sums[:, :head_dim], total, logs)
+        largest = total if r == 0 else jnp.maximum(largest, total)
+    send_lse.start()
+    again = jnp.logical_not(jnp.max(largest) <= TOTAL_MAX)
+    end()
+
+    @pl.when(again)
+    def _():
+        own_keys, far_keys = block_of(held_ref, own_side, 0), block_of(held_ref, 1 - own_side, 0)
+        beside_ones(block_of(held_ref, own_side, 1), own_ref)
+        beside_ones(block_of(held_ref, 1 - own_side, 1), far_ref)
+        for r in range(tiles):
+            products = products_of(r, q_ref, own_keys, far_keys)
+            parts = parts_of(r, pos, products, starts_ref[r * ROWS : (r + 1) * ROWS, :1], own_ref, far_ref)
+            parts.append((scores_of(r, products_with(r)), both_ref[...]))
+            shift = top_of(*[scores for scores, _ in parts]) * TO_LOG2
+            sums = sum(weigh(scores, values, shift) for scores, values in parts)
+            finish(r, sums[:, :head_dim], sums[:, head_dim:], shift)
+        send_lse.start()
+        end()
 
 
 def row_of(column):
@@ -162,9 +204,11 @@
             jax.ShapeDtypeStruct((span, head_dim), jnp.bfloat16),
             jax.ShapeDtypeStruct((1, span), jnp.float32),
         ),
-        in_specs=[SMEM, VMEM, VMEM, VMEM, VMEM, VMEM],
+        in_specs=[SMEM, VMEM, VMEM, VMEM, VMEM, VMEM, VMEM],
         out_specs=(HBM, HBM),
         scratch_shapes=[
+            both,
+            both,
             both,
             pltpu.VMEM((span, head_dim), jnp.bfloat16),
             pltpu.VMEM((1, span), jnp.float32),
@@ -172,7 +216,7 @@
         ],
         compiler_params=params,
         cost_estimate=cost(1),
-    )(pos, queries, starts, other, mixed, logs)
+    )(pos, queries, starts, held, other, mixed, logs)
 
 
 def body(queries, keys, values, doc_start):

time: 40.2 us -> 39.6 us (0.985)
  Pallas kernels: 5.51 us -> 4.91 us
    pallas_call x1, Pallas kernels: 2.63 us -> 2.21 us  [attend(): pl.pallas_call(second_kernel, out_shape=(jax.ShapeDtypeStruct((span, head...]
where the time goes in v6:
time: 39.6 us; the launch traced here: 39.3 us
  blocking collectives  23.1 us (58%)
  starting transfers between devices  9.42 us (24%)
  Pallas kernels  4.91 us (12%)
  other arithmetic  1.01 us (3%)
  between operations  0.72 us (2%)
    all_to_all x1, blocking collectives, body(): lax.all_to_all(sent.reshape((4 * width,) + own.shape), AXES, 0, 0, axis_i...  23.1 us
    ppermute x1, starting transfers between devices, body(): other = lax.ppermute(held, 'seq', [(i, i ^ 1) for i in range(count)])  8.77 us
    pallas_call x1, Pallas kernels, attend(): pl.pallas_call(first_kernel, out_shape=(state, state, jax.ShapeDtypeStruc...  2.69 us
    pallas_call x1, Pallas kernels, attend(): pl.pallas_call(second_kernel, out_shape=(jax.ShapeDtypeStruct((span, head...  2.21 us
    select_n x1, other arithmetic, body(): jnp.where(lax.broadcasted_iota(jnp.int32, (2, shard, head_dim), 0) == 0,...  0.86 us
  transfers between devices with their start and end apart: 2, of which 0 were waited for; matrix products, arithmetic and copies ran while one was open for 0% of the time, Pallas kernels for 7%

profile of v6, /device:TPU:1, one launch (start us, length us, event | category | flops | bytes accessed | tf_op | source)
XLA Modules:
  0.0 39.3 jit_solution(16737698953795801950)
XLA Ops:
  0.6 0.9 %broadcast_select_fusion.1 = bf16[2,128,128]{2,1,0:T(8,128)(2,1)S(1)} fusion(pred[2]{0:T(512)(128)(4,1)S(1)} %iota_compare_fusion, bf16[128,128]{1,0:T(8,128)(2,1)} %param.6, bf16[128,128]{1,0:T(8,128)(2,1)} %param.5), kind=kLoop, calls=%fused_computation.1 | loop fusion | flops 32768 | bytes 131074 | tf_op jit(solution)/shard_map/jit(_where)/select_n | solution.py:227
  1.5 0.7 %collective-permute-start = (bf16[2,128,128]{2,1,0:T(8,128)(2,1)S(1)}, bf16[2,128,128]{2,1,0:T(8,128)(2,1)S(1)}, u32[]{:S(2)}, u32[]{:S(2)}) collective-permute-start(bf16[2,128,128]{2,1,0:T(8,128)(2,1)S(1)} %broadcast_select_fusion.1), channel_id=1, source_target_pairs={{16,48},{24,56},{48,80},{56,88},{80,112},{88,120},{112,144},{120,1... | collective-permute-start | bytes 196616 | tf_op jit(solution)/shard_map/ppermute | solution.py:229
  2.2 0.1 iota.15
  2.3 0.1 and.21
  2.3 0.0 collective-permute-done
  2.4 0.1 broadcast_select_fusion
  2.5 0.0 copy-start
  2.5 23.1 %all_to_all.5 = bf16[16,2,128,128]{3,2,1,0:T(8,128)(2,1)S(1)} all-to-all(bf16[16,2,128,128]{3,2,1,0:T(8,128)(2,1)S(1)} %broadcast_select_fusion), channel_id=1, replica_groups={{0,1,2,3,16,17,18,19,4,5,6,7,20,21,22,23},{8,9,10,11,24,25,26,27,12,13,..., dimensions={0} | all-to-all | bytes 2097152 | tf_op jit(solution)/shard_map/all_to_all | solution.py:237
  25.6 0.0 copy-start.1
  25.6 8.8 %collective-permute-start.1 = (bf16[2,2,4,2,128,128]{5,4,3,2,1,0:T(8,128)(2,1)S(1)}, bf16[2,2,4,2,128,128]{5,4,3,2,1,0:T(8,128)(2,1)S(1)}, u32[]{:S(2)}, u32[]{:S(2)}) collective-permute-start(bf16[2,2,4,2,128,128]{5,4,3,2,1,0:T(8,128)(2,1)S(1)} %bitcast.3), channel_id=1, source_target_pairs={{0,8},{8,0},{16,24},{24,16},{32,40},{40,32},{48,56},{56,48},{64,72... | collective-permute-start | bytes 3145736 | tf_op jit(solution)/shard_map/ppermute | solution.py:239
  34.4 0.0 copy-done
  34.4 0.0 copy-done.1
  34.4 2.7 %shard_map.59 = (f32[1024,128]{1,0:T(8,128)S(1)}, f32[1024,128]{1,0:T(8,128)S(1)}, s32[1024,128]{1,0:T(8,128)S(1)}) custom-call(s32[1]{0:T(128)} %bitcast.pos_ref, bf16[1024,128]{1,0:T(8,128)(2,1)S(1)} %copy-done, s32[1,1024]{1,0:T(1,128)S(1)} %bitcast.6, bf16[2,2,4,2,128,128]{5,4,3,2,1,0:T(8,128)(2,1)S(1)} %bitcast.4), custom_call_target="tpu_custom_call" | custom-call | flops 1073741824 | bytes 3145728 | tf_op jit(solution)/shard_map/pallas_call | solution.py:192
  37.1 0.0 collective-permute-done.1.other_ref
  37.1 2.2 %shard_map.60 = (bf16[1024,128]{1,0:T(8,128)(2,1)}, f32[1,1024]{1,0:T(1,128)}) custom-call(s32[1]{0:T(128)} %bitcast.pos_ref, bf16[1024,128]{1,0:T(8,128)(2,1)S(1)} %copy-done, s32[1024,128]{1,0:T(8,128)S(1)} %get-tuple-element.5.starts_ref, bf16[2,2,4,2,128,128]{5,4,3,2,1,0:T(8,128)(2,1)S(1)} %bitcast.5, ...), custom_call_target="tpu_custom_call" | custom-call | flops 536870912 | bytes 3145728 | tf_op jit(solution)/shard_map/pallas_call | solution.py:201
  (2 shorter events, 0.0 us)
Async XLA Ops:
  1.5 0.9 %collective-permute-start = (bf16[2,128,128]{2,1,0:T(8,128)(2,1)S(1)}, bf16[2,128,128]{2,1,0:T(8,128)(2,1)S(1)}, u32[]{:S(2)}, u32[]{:S(2)}) collective-permute-start(bf16[2,128,128]{2,1,0:T(8,128)(2,1)S(1)} %broadcast_select_fusion.1), channel_id=1, source_target_pairs={{16,48},{24,56},{48,80},{56,88},{80,112},{88,120},{112,144},{120,1... | collective-permute-start | bytes 196616 | tf_op jit(solution)/shard_map/ppermute | solution.py:229
  2.5 31.9 %copy-start = (bf16[1024,128]{1,0:T(8,128)(2,1)S(1)}, bf16[1024,128]{1,0:T(8,128)(2,1)}, u32[]{:S(2)}) copy-start(bf16[1024,128]{1,0:T(8,128)(2,1)} %q_ref.3) | copy-start | bytes 786436
  25.6 8.8 %copy-start.1 = (s32[1024]{0:T(1024)S(1)}, s32[1024]{0:T(1024)}, u32[]{:S(2)}) copy-start(s32[1024]{0:T(1024)} %param.7) | copy-start | bytes 12292
  25.6 11.5 %collective-permute-start.1 = (bf16[2,2,4,2,128,128]{5,4,3,2,1,0:T(8,128)(2,1)S(1)}, bf16[2,2,4,2,128,128]{5,4,3,2,1,0:T(8,128)(2,1)S(1)}, u32[]{:S(2)}, u32[]{:S(2)}) collective-permute-start(bf16[2,2,4,2,128,128]{5,4,3,2,1,0:T(8,128)(2,1)S(1)} %bitcast.3), channel_id=1, source_target_pairs={{0,8},{8,0},{16,24},{24,16},{32,40},{40,32},{48,56},{56,48},{64,72... | collective-permute-start | bytes 3145736 | tf_op jit(solution)/shard_map/ppermute | solution.py:239

commit v7 on v6

--- a/solution.py
+++ b/solution.py
@@ -52,8 +52,10 @@
 
 
 def block_of(ref, side, kind):
-    rows = ref.shape[0] * ref.shape[2] * ref.shape[4]
-    return ref[:, side, :, kind].reshape(rows, ref.shape[5])
+    highs, width = ref.shape[0], ref.shape[2]
+    half = width // 2
+    at = [y + side * (half if y < half else -half) for y in range(width)]
+    return jnp.concatenate([ref[high, side, at[y], kind] for high in range(highs) for y in range(width)], axis=0)
 
 
 def query_positions(pos, r, span):
@@ -230,7 +232,12 @@
     to_side = lax.broadcasted_iota(jnp.int32, (2, 2, width) + own.shape, 1)
     sent = jnp.where((to_side == 0) & (pos % 4 >= 2), below, own)
     slabs = [
-        [(z * 4 + side * 2 + core) * heads + high * width + y for high in range(2) for side in range(2) for y in range(width)]
+        [
+            (z * 4 + side * 2 + core) * heads + high * width + (y + side * (width // 2)) % width
+            for high in range(2)
+            for side in range(2)
+            for y in range(width)
+        ]
         for z in range(count // 4)
         for core in range(2)
     ]

time: 39.6 us -> 39 us (0.985)
  blocking collectives: 23.1 us -> 22.5 us
    all_to_all x1, blocking collectives: 23.1 us -> 22.5 us  [body(): lax.all_to_all(sent.reshape((4 * width,) + own.shape), AXES, 0, 0, axis_i...]
where the time goes in v7:
time: 39 us; the launch traced here: 38.6 us
  blocking collectives  22.5 us (58%)
  starting transfers between devices  9.25 us (24%)
  Pallas kernels  4.93 us (13%)
  other arithmetic  1.01 us (3%)
  between operations  0.72 us (2%)
    all_to_all x1, blocking collectives, body(): lax.all_to_all(sent.reshape((4 * width,) + own.shape), AXES, 0, 0, axis_i...  22.5 us
    ppermute x1, starting transfers between devices, body(): other = lax.ppermute(held, 'seq', [(i, i ^ 1) for i in range(count)])  8.59 us
    pallas_call x1, Pallas kernels, attend(): pl.pallas_call(first_kernel, out_shape=(state, state, jax.ShapeDtypeStruc...  2.72 us
    pallas_call x1, Pallas kernels, attend(): pl.pallas_call(second_kernel, out_shape=(jax.ShapeDtypeStruct((span, head...  2.21 us
    select_n x1, other arithmetic, body(): jnp.where(lax.broadcasted_iota(jnp.int32, (2, shard, head_dim), 0) == 0,...  0.86 us
  transfers between devices with their start and end apart: 2, of which 0 were waited for; matrix products, arithmetic and copies ran while one was open for 0% of the time, Pallas kernels for 7%

profile of v7, /device:TPU:1, one launch (start us, length us, event | category | flops | bytes accessed | tf_op | source)
XLA Modules:
  0.0 38.6 jit_solution(8316631368731728111)
XLA Ops:
  0.6 0.9 %broadcast_select_fusion.1 = bf16[2,128,128]{2,1,0:T(8,128)(2,1)S(1)} fusion(pred[2]{0:T(512)(128)(4,1)S(1)} %iota_compare_fusion, bf16[128,128]{1,0:T(8,128)(2,1)} %param.6, bf16[128,128]{1,0:T(8,128)(2,1)} %param.5), kind=kLoop, calls=%fused_computation.1 | loop fusion | flops 32768 | bytes 131074 | tf_op jit(solution)/shard_map/jit(_where)/select_n | solution.py:229
  1.5 0.7 %collective-permute-start = (bf16[2,128,128]{2,1,0:T(8,128)(2,1)S(1)}, bf16[2,128,128]{2,1,0:T(8,128)(2,1)S(1)}, u32[]{:S(2)}, u32[]{:S(2)}) collective-permute-start(bf16[2,128,128]{2,1,0:T(8,128)(2,1)S(1)} %broadcast_select_fusion.1), channel_id=1, source_target_pairs={{16,48},{24,56},{48,80},{56,88},{80,112},{88,120},{112,144},{120,1... | collective-permute-start | bytes 196616 | tf_op jit(solution)/shard_map/ppermute | solution.py:231
  2.2 0.1 iota.15
  2.3 0.1 and.21
  2.3 0.0 collective-permute-done
  2.4 0.1 broadcast_select_fusion
  2.5 0.0 copy-start
  2.5 22.5 %all_to_all.5 = bf16[16,2,128,128]{3,2,1,0:T(8,128)(2,1)S(1)} all-to-all(bf16[16,2,128,128]{3,2,1,0:T(8,128)(2,1)S(1)} %broadcast_select_fusion), channel_id=1, replica_groups={{0,1,2,3,18,19,16,17,4,5,6,7,22,23,20,21},{8,9,10,11,26,27,24,25,12,13,..., dimensions={0} | all-to-all | bytes 2097152 | tf_op jit(solution)/shard_map/all_to_all | solution.py:244
  25.0 0.0 copy-start.1
  25.0 8.6 %collective-permute-start.1 = (bf16[2,2,4,2,128,128]{5,4,3,2,1,0:T(8,128)(2,1)S(1)}, bf16[2,2,4,2,128,128]{5,4,3,2,1,0:T(8,128)(2,1)S(1)}, u32[]{:S(2)}, u32[]{:S(2)}) collective-permute-start(bf16[2,2,4,2,128,128]{5,4,3,2,1,0:T(8,128)(2,1)S(1)} %bitcast.3), channel_id=1, source_target_pairs={{0,8},{8,0},{16,24},{24,16},{32,40},{40,32},{48,56},{56,48},{64,72... | collective-permute-start | bytes 3145736 | tf_op jit(solution)/shard_map/ppermute | solution.py:246
  33.6 0.0 copy-done
  33.7 0.0 copy-done.1
  33.7 2.7 %shard_map.59 = (f32[1024,128]{1,0:T(8,128)S(1)}, f32[1024,128]{1,0:T(8,128)S(1)}, s32[1024,128]{1,0:T(8,128)S(1)}) custom-call(s32[1]{0:T(128)} %bitcast.pos_ref, bf16[1024,128]{1,0:T(8,128)(2,1)S(1)} %copy-done, s32[1,1024]{1,0:T(1,128)S(1)} %bitcast.6, bf16[2,2,4,2,128,128]{5,4,3,2,1,0:T(8,128)(2,1)S(1)} %bitcast.4), custom_call_target="tpu_custom_call" | custom-call | flops 1073741824 | bytes 3145728 | tf_op jit(solution)/shard_map/pallas_call | solution.py:194
  36.4 0.0 collective-permute-done.1.other_ref
  36.4 2.2 %shard_map.60 = (bf16[1024,128]{1,0:T(8,128)(2,1)}, f32[1,1024]{1,0:T(1,128)}) custom-call(s32[1]{0:T(128)} %bitcast.pos_ref, bf16[1024,128]{1,0:T(8,128)(2,1)S(1)} %copy-done, s32[1024,128]{1,0:T(8,128)S(1)} %get-tuple-element.5.starts_ref, bf16[2,2,4,2,128,128]{5,4,3,2,1,0:T(8,128)(2,1)S(1)} %bitcast.5, ...), custom_call_target="tpu_custom_call" | custom-call | flops 536870912 | bytes 3145728 | tf_op jit(solution)/shard_map/pallas_call | solution.py:203
  (2 shorter events, 0.0 us)
Async XLA Ops:
  1.5 0.9 %collective-permute-start = (bf16[2,128,128]{2,1,0:T(8,128)(2,1)S(1)}, bf16[2,128,128]{2,1,0:T(8,128)(2,1)S(1)}, u32[]{:S(2)}, u32[]{:S(2)}) collective-permute-start(bf16[2,128,128]{2,1,0:T(8,128)(2,1)S(1)} %broadcast_select_fusion.1), channel_id=1, source_target_pairs={{16,48},{24,56},{48,80},{56,88},{80,112},{88,120},{112,144},{120,1... | collective-permute-start | bytes 196616 | tf_op jit(solution)/shard_map/ppermute | solution.py:231
  2.5 31.1 %copy-start = (bf16[1024,128]{1,0:T(8,128)(2,1)S(1)}, bf16[1024,128]{1,0:T(8,128)(2,1)}, u32[]{:S(2)}) copy-start(bf16[1024,128]{1,0:T(8,128)(2,1)} %q_ref.3) | copy-start | bytes 786436
  25.0 8.6 %copy-start.1 = (s32[1024]{0:T(1024)S(1)}, s32[1024]{0:T(1024)}, u32[]{:S(2)}) copy-start(s32[1024]{0:T(1024)} %param.7) | copy-start | bytes 12292
  25.0 11.4 %collective-permute-start.1 = (bf16[2,2,4,2,128,128]{5,4,3,2,1,0:T(8,128)(2,1)S(1)}, bf16[2,2,4,2,128,128]{5,4,3,2,1,0:T(8,128)(2,1)S(1)}, u32[]{:S(2)}, u32[]{:S(2)}) collective-permute-start(bf16[2,2,4,2,128,128]{5,4,3,2,1,0:T(8,128)(2,1)S(1)} %bitcast.3), channel_id=1, source_target_pairs={{0,8},{8,0},{16,24},{24,16},{32,40},{40,32},{48,56},{56,48},{64,72... | collective-permute-start | bytes 3145736 | tf_op jit(solution)/shard_map/ppermute | solution.py:246

commit v8 on v7

--- a/solution.py
+++ b/solution.py
@@ -51,10 +51,11 @@
     both_ref[:, head_dim:] = jnp.ones_like(values)
 
 
-def block_of(ref, side, kind):
+def block_of(ref, side, kind, core):
     highs, width = ref.shape[0], ref.shape[2]
     half = width // 2
-    at = [y + side * (half if y < half else -half) for y in range(width)]
+    turned = lax.rem(side + core, 2)
+    at = [y + turned * (half if y < half else -half) for y in range(width)]
     return jnp.concatenate([ref[high, side, at[y], kind] for high in range(highs) for y in range(width)], axis=0)
 
 
@@ -82,13 +83,13 @@
 def first_kernel(pos_ref, q_ref, start_ref, held_ref, mixed_ref, log_ref, starts_ref, row_ref, own_ref, far_ref, sem):
     span, head_dim = q_ref.shape
     pos = pos_ref[0]
-    side = lax.rem(pos // 2, 2)
+    side, core = lax.rem(pos // 2, 2), lax.rem(pos, 2)
     fetch = pltpu.make_async_copy(start_ref, row_ref, sem)
     fetch.start()
-    own_keys, far_keys = block_of(held_ref, side, 0), block_of(held_ref, 1 - side, 0)
+    own_keys, far_keys = block_of(held_ref, side, 0, core), block_of(held_ref, 1 - side, 0, core)
     upcoming = products_of(0, q_ref, own_keys, far_keys)
-    beside_ones(block_of(held_ref, side, 1), own_ref)
-    beside_ones(block_of(held_ref, 1 - side, 1), far_ref)
+    beside_ones(block_of(held_ref, side, 1, core), own_ref)
+    beside_ones(block_of(held_ref, 1 - side, 1, core), far_ref)
     with_own = jnp.sum(q_ref[...].astype(jnp.float32) * own_keys.astype(jnp.float32), axis=1, keepdims=True)
     log_ref[...] = jnp.broadcast_to(with_own * TO_LOG2, log_ref.shape)
     fetch.wait()
@@ -113,7 +114,7 @@
     pos = pos_ref[0]
     own_side, odd = lax.rem(pos // 2, 2), lax.rem(pos, 2)
     side = jnp.where(odd == 1, own_side, 1 - own_side)
-    keys = block_of(other_ref, side, 0)
+    keys = block_of(other_ref, side, 0, 1 - odd)
     tiles = span // ROWS
 
     def products_with(r):
@@ -139,7 +140,7 @@
             send(r).wait()
         send_lse.wait()
 
-    beside_ones(block_of(other_ref, side, 1), both_ref)
+    beside_ones(block_of(other_ref, side, 1, 1 - odd), both_ref)
     largest = None
     for r in range(tiles):
         rows = slice(r * ROWS, (r + 1) * ROWS)
@@ -155,9 +156,9 @@
 
     @pl.when(again)
     def _():
-        own_keys, far_keys = block_of(held_ref, own_side, 0), block_of(held_ref, 1 - own_side, 0)
-        beside_ones(block_of(held_ref, own_side, 1), own_ref)
-        beside_ones(block_of(held_ref, 1 - own_side, 1), far_ref)
+        own_keys, far_keys = block_of(held_ref, own_side, 0, odd), block_of(held_ref, 1 - own_side, 0, odd)
+        beside_ones(block_of(held_ref, own_side, 1, odd), own_ref)
+        beside_ones(block_of(held_ref, 1 - own_side, 1, odd), far_ref)
         for r in range(tiles):
             products = products_of(r, q_ref, own_keys, far_keys)
             parts = parts_of(r, pos, products, starts_ref[r * ROWS : (r + 1) * ROWS, :1], own_ref, far_ref)
@@ -233,7 +234,7 @@
     sent = jnp.where((to_side == 0) & (pos % 4 >= 2), below, own)
     slabs = [
         [
-            (z * 4 + side * 2 + core) * heads + high * width + (y + side * (width // 2)) % width
+            (z * 4 + side * 2 + core) * heads + high * width + (y + (side + core) * (width // 2)) % width
             for high in range(2)
             for side in range(2)
             for y in range(width)

time: 39 us -> 38.9 us (level)
  starting transfers between devices: 9.25 us -> 9.87 us
  blocking collectives: 22.5 us -> 21.9 us
    ppermute x1, starting transfers between devices: 8.59 us -> 9.22 us  [body(): other = lax.ppermute(held, 'seq', [(i, i ^ 1) for i in range(count)])]
    all_to_all x1, blocking collectives: 22.5 us -> 21.9 us  [body(): lax.all_to_all(sent.reshape((4 * width,) + own.shape), AXES, 0, 0, axis_i...]
where the time goes in v8:
time: 38.9 us; the launch traced here: 38.6 us
  blocking collectives  21.9 us (56%)
  starting transfers between devices  9.87 us (25%)
  Pallas kernels  4.91 us (13%)
  other arithmetic  1.01 us (3%)
  between operations  0.72 us (2%)
    all_to_all x1, blocking collectives, body(): lax.all_to_all(sent.reshape((4 * width,) + own.shape), AXES, 0, 0, axis_i...  21.9 us
    ppermute x1, starting transfers between devices, body(): other = lax.ppermute(held, 'seq', [(i, i ^ 1) for i in range(count)])  9.22 us
    pallas_call x1, Pallas kernels, attend(): pl.pallas_call(first_kernel, out_shape=(state, state, jax.ShapeDtypeStruc...  2.7 us
    pallas_call x1, Pallas kernels, attend(): pl.pallas_call(second_kernel, out_shape=(jax.ShapeDtypeStruct((span, head...  2.21 us
    select_n x1, other arithmetic, body(): jnp.where(lax.broadcasted_iota(jnp.int32, (2, shard, head_dim), 0) == 0,...  0.86 us
  transfers between devices with their start and end apart: 2, of which 0 were waited for; matrix products, arithmetic and copies ran while one was open for 0% of the time, Pallas kernels for 7%

profile of v8, /device:TPU:1, one launch (start us, length us, event | category | flops | bytes accessed | tf_op | source)
XLA Modules:
  0.0 38.6 jit_solution(12501181787947794567)
XLA Ops:
  0.6 0.9 %broadcast_select_fusion.1 = bf16[2,128,128]{2,1,0:T(8,128)(2,1)S(1)} fusion(pred[2]{0:T(512)(128)(4,1)S(1)} %iota_compare_fusion, bf16[128,128]{1,0:T(8,128)(2,1)} %param.6, bf16[128,128]{1,0:T(8,128)(2,1)} %param.5), kind=kLoop, calls=%fused_computation.1 | loop fusion | flops 32768 | bytes 131074 | tf_op jit(solution)/shard_map/jit(_where)/select_n | solution.py:230
  1.5 0.7 %collective-permute-start = (bf16[2,128,128]{2,1,0:T(8,128)(2,1)S(1)}, bf16[2,128,128]{2,1,0:T(8,128)(2,1)S(1)}, u32[]{:S(2)}, u32[]{:S(2)}) collective-permute-start(bf16[2,128,128]{2,1,0:T(8,128)(2,1)S(1)} %broadcast_select_fusion.1), channel_id=1, source_target_pairs={{16,48},{24,56},{48,80},{56,88},{80,112},{88,120},{112,144},{120,1... | collective-permute-start | bytes 196616 | tf_op jit(solution)/shard_map/ppermute | solution.py:232
  2.2 0.1 iota.15
  2.3 0.1 and.21
  2.3 0.0 collective-permute-done
  2.4 0.1 broadcast_select_fusion
  2.5 0.0 copy-start
  2.5 21.9 %all_to_all.5 = bf16[16,2,128,128]{3,2,1,0:T(8,128)(2,1)S(1)} all-to-all(bf16[16,2,128,128]{3,2,1,0:T(8,128)(2,1)S(1)} %broadcast_select_fusion), channel_id=1, replica_groups={{0,1,2,3,18,19,16,17,4,5,6,7,22,23,20,21},{10,11,8,9,24,25,26,27,14,15,..., dimensions={0} | all-to-all | bytes 2097152 | tf_op jit(solution)/shard_map/all_to_all | solution.py:245
  24.4 0.0 copy-start.1
  24.4 9.2 %collective-permute-start.1 = (bf16[2,2,4,2,128,128]{5,4,3,2,1,0:T(8,128)(2,1)S(1)}, bf16[2,2,4,2,128,128]{5,4,3,2,1,0:T(8,128)(2,1)S(1)}, u32[]{:S(2)}, u32[]{:S(2)}) collective-permute-start(bf16[2,2,4,2,128,128]{5,4,3,2,1,0:T(8,128)(2,1)S(1)} %bitcast.3), channel_id=1, source_target_pairs={{0,8},{8,0},{16,24},{24,16},{32,40},{40,32},{48,56},{56,48},{64,72... | collective-permute-start | bytes 3145736 | tf_op jit(solution)/shard_map/ppermute | solution.py:247
  33.6 0.0 copy-done
  33.7 0.0 copy-done.1
  33.7 2.7 %shard_map.59 = (f32[1024,128]{1,0:T(8,128)S(1)}, f32[1024,128]{1,0:T(8,128)S(1)}, s32[1024,128]{1,0:T(8,128)S(1)}) custom-call(s32[1]{0:T(128)} %bitcast.pos_ref, bf16[1024,128]{1,0:T(8,128)(2,1)S(1)} %copy-done, s32[1,1024]{1,0:T(1,128)S(1)} %bitcast.6, bf16[2,2,4,2,128,128]{5,4,3,2,1,0:T(8,128)(2,1)S(1)} %bitcast.4), custom_call_target="tpu_custom_call" | custom-call | flops 1073741824 | bytes 3145728 | tf_op jit(solution)/shard_map/pallas_call | solution.py:195
  36.4 0.0 collective-permute-done.1.other_ref
  36.4 2.2 %shard_map.60 = (bf16[1024,128]{1,0:T(8,128)(2,1)}, f32[1,1024]{1,0:T(1,128)}) custom-call(s32[1]{0:T(128)} %bitcast.pos_ref, bf16[1024,128]{1,0:T(8,128)(2,1)S(1)} %copy-done, s32[1024,128]{1,0:T(8,128)S(1)} %get-tuple-element.5.starts_ref, bf16[2,2,4,2,128,128]{5,4,3,2,1,0:T(8,128)(2,1)S(1)} %bitcast.5, ...), custom_call_target="tpu_custom_call" | custom-call | flops 536870912 | bytes 3145728 | tf_op jit(solution)/shard_map/pallas_call | solution.py:204
  (2 shorter events, 0.0 us)
Async XLA Ops:
  1.5 0.9 %collective-permute-start = (bf16[2,128,128]{2,1,0:T(8,128)(2,1)S(1)}, bf16[2,128,128]{2,1,0:T(8,128)(2,1)S(1)}, u32[]{:S(2)}, u32[]{:S(2)}) collective-permute-start(bf16[2,128,128]{2,1,0:T(8,128)(2,1)S(1)} %broadcast_select_fusion.1), channel_id=1, source_target_pairs={{16,48},{24,56},{48,80},{56,88},{80,112},{88,120},{112,144},{120,1... | collective-permute-start | bytes 196616 | tf_op jit(solution)/shard_map/ppermute | solution.py:232
  2.5 31.1 %copy-start = (bf16[1024,128]{1,0:T(8,128)(2,1)S(1)}, bf16[1024,128]{1,0:T(8,128)(2,1)}, u32[]{:S(2)}) copy-start(bf16[1024,128]{1,0:T(8,128)(2,1)} %q_ref.3) | copy-start | bytes 786436
  24.4 9.2 %copy-start.1 = (s32[1024]{0:T(1024)S(1)}, s32[1024]{0:T(1024)}, u32[]{:S(2)}) copy-start(s32[1024]{0:T(1024)} %param.7) | copy-start | bytes 12292
  24.4 12.0 %collective-permute-start.1 = (bf16[2,2,4,2,128,128]{5,4,3,2,1,0:T(8,128)(2,1)S(1)}, bf16[2,2,4,2,128,128]{5,4,3,2,1,0:T(8,128)(2,1)S(1)}, u32[]{:S(2)}, u32[]{:S(2)}) collective-permute-start(bf16[2,2,4,2,128,128]{5,4,3,2,1,0:T(8,128)(2,1)S(1)} %bitcast.3), channel_id=1, source_target_pairs={{0,8},{8,0},{16,24},{24,16},{32,40},{40,32},{48,56},{56,48},{64,72... | collective-permute-start | bytes 3145736 | tf_op jit(solution)/shard_map/ppermute | solution.py:247

commit v9 on v8

--- a/solution.py
+++ b/solution.py
@@ -80,7 +80,7 @@
     return parts
 
 
-def first_kernel(pos_ref, q_ref, start_ref, held_ref, mixed_ref, log_ref, starts_ref, row_ref, own_ref, far_ref, sem):
+def first_kernel(pos_ref, q_ref, start_ref, held_ref, sums_ref, shift_ref, starts_ref, row_ref, own_ref, far_ref, sem):
     span, head_dim = q_ref.shape
     pos = pos_ref[0]
     side, core = lax.rem(pos // 2, 2), lax.rem(pos, 2)
@@ -91,7 +91,7 @@
     beside_ones(block_of(held_ref, side, 1, core), own_ref)
     beside_ones(block_of(held_ref, 1 - side, 1, core), far_ref)
     with_own = jnp.sum(q_ref[...].astype(jnp.float32) * own_keys.astype(jnp.float32), axis=1, keepdims=True)
-    log_ref[...] = jnp.broadcast_to(with_own * TO_LOG2, log_ref.shape)
+    shift_ref[...] = jnp.broadcast_to(with_own * TO_LOG2, shift_ref.shape)
     fetch.wait()
     starts_ref[...] = jnp.broadcast_to(row_ref[...], (head_dim, span)).T
     for r in range(span // ROWS):
@@ -99,16 +99,13 @@
         products = upcoming
         if (r + 1) * ROWS < span:
             upcoming = products_of(r + 1, q_ref, own_keys, far_keys)
-        shift = log_ref[rows, :]
+        shift = shift_ref[rows, :]
         parts = parts_of(r, pos, products, starts_ref[rows, :1], own_ref, far_ref)
-        sums = sum(weigh(scores, values, shift[:, :1]) for scores, values in parts)
-        total = sums[:, head_dim:]
-        mixed_ref[rows, :] = sums[:, :head_dim] / total
-        log_ref[rows, :] = jnp.where(total <= TOTAL_MAX, shift + jnp.log2(total), -jnp.inf)
+        sums_ref[rows, :] = sum(weigh(scores, values, shift[:, :1]) for scores, values in parts)
 
 
 def second_kernel(
-    pos_ref, q_ref, starts_ref, held_ref, other_ref, mixed_ref, log_ref, out_ref, lse_ref, both_ref, own_ref, far_ref, out_vmem, lse_vmem, sems
+    pos_ref, q_ref, starts_ref, held_ref, other_ref, sums_ref, shift_ref, out_ref, lse_ref, both_ref, own_ref, far_ref, out_vmem, lse_vmem, sems
 ):
     span, head_dim = q_ref.shape
     pos = pos_ref[0]
@@ -129,9 +126,9 @@
 
     send_lse = pltpu.make_async_copy(lse_vmem, lse_ref, sems.at[tiles])
 
-    def finish(r, mixed, total, shift):
-        rows = slice(r * ROWS, (r + 1) * ROWS)
-        out_vmem[rows, :] = (mixed / total).astype(out_ref.dtype)
+    def finish(r, sums, shift):
+        rows, total = slice(r * ROWS, (r + 1) * ROWS), sums[:, head_dim:]
+        out_vmem[rows, :] = (sums[:, :head_dim] / total).astype(out_ref.dtype)
         send(r).start()
         lse_vmem[:, rows] = row_of((shift + jnp.log2(total)) * LN2)
 
@@ -145,10 +142,10 @@
     for r in range(tiles):
         rows = slice(r * ROWS, (r + 1) * ROWS)
         products = products_with(r)
-        logs = log_ref[rows, :]
-        sums = weigh(scores_of(r, products), both_ref[...], logs)
-        total = sums[:, head_dim:] + 1.0
-        finish(r, mixed_ref[rows, :] + sums[:, :head_dim], total, logs)
+        shift = shift_ref[rows, :]
+        sums = sums_ref[rows, :] + weigh(scores_of(r, products), both_ref[...], shift)
+        finish(r, sums, shift)
+        total = sums[:, head_dim:]
         largest = total if r == 0 else jnp.maximum(largest, total)
     send_lse.start()
     again = jnp.logical_not(jnp.max(largest) <= TOTAL_MAX)
@@ -165,7 +162,7 @@
             parts.append((scores_of(r, products_with(r)), both_ref[...]))
             shift = top_of(*[scores for scores, _ in parts]) * TO_LOG2
             sums = sum(weigh(scores, values, shift) for scores, values in parts)
-            finish(r, sums[:, :head_dim], sums[:, head_dim:], shift)
+            finish(r, sums, shift)
         send_lse.start()
         end()
 
@@ -181,7 +178,6 @@
 
 def attend(pos, queries, doc_start, held, other):
     span, head_dim = queries.shape
-    state = jax.ShapeDtypeStruct((span, head_dim), jnp.float32)
     params = pltpu.CompilerParams(vmem_limit_bytes=VMEM_LIMIT)
     both = pltpu.VMEM((span, 2 * head_dim), jnp.bfloat16)
 
@@ -192,9 +188,13 @@
             transcendentals=blocks * span * span,
         )
 
-    mixed, logs, starts = pl.pallas_call(
+    sums, shift, starts = pl.pallas_call(
         first_kernel,
-        out_shape=(state, state, jax.ShapeDtypeStruct((span, head_dim), jnp.int32)),
+        out_shape=(
+            jax.ShapeDtypeStruct((span, 2 * head_dim), jnp.float32),
+            jax.ShapeDtypeStruct((span, head_dim), jnp.float32),
+            jax.ShapeDtypeStruct((span, head_dim), jnp.int32),
+        ),
         in_specs=[SMEM, VMEM, HBM, VMEM],
         out_specs=(VMEM, VMEM, VMEM),
         scratch_shapes=[pltpu.VMEM((1, span), jnp.int32), both, both, pltpu.SemaphoreType.DMA],
@@ -219,7 +219,7 @@
         ],
         compiler_params=params,
         cost_estimate=cost(1),
-    )(pos, queries, starts, held, other, mixed, logs)
+    )(pos, queries, starts, held, other, sums, shift)
 
 
 def body(queries, keys, values, doc_start):

time: 38.9 us -> 38.9 us (level)
  no operation moved by 1% of the time
where the time goes in v9:
time: 38.9 us; the launch traced here: 38.6 us
  blocking collectives  21.9 us (56%)
  starting transfers between devices  9.87 us (25%)
  Pallas kernels  4.9 us (13%)
  other arithmetic  1.01 us (3%)
  between operations  0.72 us (2%)
    all_to_all x1, blocking collectives, body(): lax.all_to_all(sent.reshape((4 * width,) + own.shape), AXES, 0, 0, axis_i...  21.9 us
    ppermute x1, starting transfers between devices, body(): other = lax.ppermute(held, 'seq', [(i, i ^ 1) for i in range(count)])  9.22 us
    pallas_call x1, Pallas kernels, attend(): pl.pallas_call(first_kernel, out_shape=(jax.ShapeDtypeStruct((span, 2 * h...  2.68 us
    pallas_call x1, Pallas kernels, attend(): pl.pallas_call(second_kernel, out_shape=(jax.ShapeDtypeStruct((span, head...  2.22 us
    select_n x1, other arithmetic, body(): jnp.where(lax.broadcasted_iota(jnp.int32, (2, shard, head_dim), 0) == 0,...  0.86 us
  transfers between devices with their start and end apart: 2, of which 0 were waited for; matrix products, arithmetic and copies ran while one was open for 0% of the time, Pallas kernels for 7%

profile of v9, /device:TPU:1, one launch (start us, length us, event | category | flops | bytes accessed | tf_op | source)
XLA Modules:
  0.0 38.6 jit_solution(3884453144783321038)
XLA Ops:
  0.6 0.9 %broadcast_select_fusion.1 = bf16[2,128,128]{2,1,0:T(8,128)(2,1)S(1)} fusion(pred[2]{0:T(512)(128)(4,1)S(1)} %iota_compare_fusion, bf16[128,128]{1,0:T(8,128)(2,1)} %param.6, bf16[128,128]{1,0:T(8,128)(2,1)} %param.5), kind=kLoop, calls=%fused_computation.1 | loop fusion | flops 32768 | bytes 131074 | tf_op jit(solution)/shard_map/jit(_where)/select_n | solution.py:230
  1.5 0.7 %collective-permute-start = (bf16[2,128,128]{2,1,0:T(8,128)(2,1)S(1)}, bf16[2,128,128]{2,1,0:T(8,128)(2,1)S(1)}, u32[]{:S(2)}, u32[]{:S(2)}) collective-permute-start(bf16[2,128,128]{2,1,0:T(8,128)(2,1)S(1)} %broadcast_select_fusion.1), channel_id=1, source_target_pairs={{16,48},{24,56},{48,80},{56,88},{80,112},{88,120},{112,144},{120,1... | collective-permute-start | bytes 196616 | tf_op jit(solution)/shard_map/ppermute | solution.py:232
  2.2 0.1 iota.15
  2.3 0.1 and.21
  2.3 0.0 collective-permute-done
  2.4 0.1 broadcast_select_fusion
  2.5 0.0 copy-start
  2.5 21.9 %all_to_all.5 = bf16[16,2,128,128]{3,2,1,0:T(8,128)(2,1)S(1)} all-to-all(bf16[16,2,128,128]{3,2,1,0:T(8,128)(2,1)S(1)} %broadcast_select_fusion), channel_id=1, replica_groups={{0,1,2,3,18,19,16,17,4,5,6,7,22,23,20,21},{10,11,8,9,24,25,26,27,14,15,..., dimensions={0} | all-to-all | bytes 2097152 | tf_op jit(solution)/shard_map/all_to_all | solution.py:245
  24.4 0.0 copy-start.1
  24.4 9.2 %collective-permute-start.1 = (bf16[2,2,4,2,128,128]{5,4,3,2,1,0:T(8,128)(2,1)S(1)}, bf16[2,2,4,2,128,128]{5,4,3,2,1,0:T(8,128)(2,1)S(1)}, u32[]{:S(2)}, u32[]{:S(2)}) collective-permute-start(bf16[2,2,4,2,128,128]{5,4,3,2,1,0:T(8,128)(2,1)S(1)} %bitcast.3), channel_id=1, source_target_pairs={{0,8},{8,0},{16,24},{24,16},{32,40},{40,32},{48,56},{56,48},{64,72... | collective-permute-start | bytes 3145736 | tf_op jit(solution)/shard_map/ppermute | solution.py:247
  33.6 0.0 copy-done
  33.7 0.0 copy-done.1
  33.7 2.7 %shard_map.59 = (f32[1024,256]{1,0:T(8,128)S(1)}, f32[1024,128]{1,0:T(8,128)S(1)}, s32[1024,128]{1,0:T(8,128)S(1)}) custom-call(s32[1]{0:T(128)} %bitcast.pos_ref, bf16[1024,128]{1,0:T(8,128)(2,1)S(1)} %copy-done, s32[1,1024]{1,0:T(1,128)S(1)} %bitcast.6, bf16[2,2,4,2,128,128]{5,4,3,2,1,0:T(8,128)(2,1)S(1)} %bitcast.4), custom_call_target="tpu_custom_call" | custom-call | flops 1073741824 | bytes 3145728 | tf_op jit(solution)/shard_map/pallas_call | solution.py:191
  36.4 0.0 collective-permute-done.1.other_ref
  36.4 2.2 %shard_map.60 = (bf16[1024,128]{1,0:T(8,128)(2,1)}, f32[1,1024]{1,0:T(1,128)}) custom-call(s32[1]{0:T(128)} %bitcast.pos_ref, bf16[1024,128]{1,0:T(8,128)(2,1)S(1)} %copy-done, s32[1024,128]{1,0:T(8,128)S(1)} %get-tuple-element.5.starts_ref, bf16[2,2,4,2,128,128]{5,4,3,2,1,0:T(8,128)(2,1)S(1)} %bitcast.5, ...), custom_call_target="tpu_custom_call" | custom-call | flops 536870912 | bytes 3145728 | tf_op jit(solution)/shard_map/pallas_call | solution.py:204
  (2 shorter events, 0.0 us)
Async XLA Ops:
  1.5 0.9 %collective-permute-start = (bf16[2,128,128]{2,1,0:T(8,128)(2,1)S(1)}, bf16[2,128,128]{2,1,0:T(8,128)(2,1)S(1)}, u32[]{:S(2)}, u32[]{:S(2)}) collective-permute-start(bf16[2,128,128]{2,1,0:T(8,128)(2,1)S(1)} %broadcast_select_fusion.1), channel_id=1, source_target_pairs={{16,48},{24,56},{48,80},{56,88},{80,112},{88,120},{112,144},{120,1... | collective-permute-start | bytes 196616 | tf_op jit(solution)/shard_map/ppermute | solution.py:232
  2.5 31.1 %copy-start = (bf16[1024,128]{1,0:T(8,128)(2,1)S(1)}, bf16[1024,128]{1,0:T(8,128)(2,1)}, u32[]{:S(2)}) copy-start(bf16[1024,128]{1,0:T(8,128)(2,1)} %q_ref.3) | copy-start | bytes 786436
  24.4 9.2 %copy-start.1 = (s32[1024]{0:T(1024)S(1)}, s32[1024]{0:T(1024)}, u32[]{:S(2)}) copy-start(s32[1024]{0:T(1024)} %param.7) | copy-start | bytes 12292
  24.4 11.9 %collective-permute-start.1 = (bf16[2,2,4,2,128,128]{5,4,3,2,1,0:T(8,128)(2,1)S(1)}, bf16[2,2,4,2,128,128]{5,4,3,2,1,0:T(8,128)(2,1)S(1)}, u32[]{:S(2)}, u32[]{:S(2)}) collective-permute-start(bf16[2,2,4,2,128,128]{5,4,3,2,1,0:T(8,128)(2,1)S(1)} %bitcast.3), channel_id=1, source_target_pairs={{0,8},{8,0},{16,24},{24,16},{32,40},{40,32},{48,56},{56,48},{64,72... | collective-permute-start | bytes 3145736 | tf_op jit(solution)/shard_map/ppermute | solution.py:247
